TPU v7x, 128 devices: a whole 4x4x4 slice. The times are simulated.
128 devices in a mesh: lat: 8 (over z_lo, y), lon: 16 (over z_hi, x, core).
Axes of the slice: x: 4, y: 4, z: 4 (z_hi: 2, z_lo: 2; z = z_hi * 2 + z_lo), core: 2. Of those that a mesh axis runs over, the one named last changes fastest.
Arguments:
- tokens: bfloat16 [8, 96, 36864], P(None, 'lat', 'lon'), may hold values from -6 to 6
- surface_ids: int32 [96, 192], P('lat', 'lon'), may hold values from 0 to 2
- surface_embed: bfloat16 [3, 192], replicated, may hold values from -5 to 5
- type_index: int32 [16], P('lat'), may hold values from 0 to 15
- bias_plain: bfloat16 [1271808], P('lon'), may hold values from -4 to 300
- bias_shift: bfloat16 [1271808], P('lon'), may hold values from -4 to 300
- w_qkv: bfloat16 [2, 110592], replicated, may hold values from -0.21875 to 0.21875
- w_proj: bfloat16 [2, 36864], replicated, may hold values from -0.875 to 0.875
- w_up: bfloat16 [2, 192, 768], replicated, may hold values from -0.4375 to 0.4375
- w_down: bfloat16 [2, 147456], replicated, may hold values from -0.21875 to 0.21875
Outputs:
- evolved: bfloat16 [8, 96, 36864], P(None, 'lat', 'lon')
All inputs are finite; a program needn't handle non-finite values.
Results may differ from a plain program's by a relative error of at most 0.015.
Values may be sent and summed in bfloat16 or wider, within the bound.
A program may use at most 128 MiB of HBM per device.

v0:
```python
import jax
import jax.numpy as jnp
from jax import lax
from jax.sharding import PartitionSpec as P

HEADS = 6
HEAD_DIM = 32
WZ = 2
WH = 6
WW = 12
RELPOS = 3312


def passed_along(block, axis, distance):
    devices = range(lax.axis_size(axis))
    route = [((i - distance) % len(devices), i) for i in devices]
    return lax.ppermute(block, axis, route)


def layer_norm(stream):
    values = stream.astype(jnp.float32)
    center = jnp.mean(values, axis=-1, keepdims=True)
    spread = jnp.mean(jnp.square(values - center), axis=-1, keepdims=True)
    return (values - center) * lax.rsqrt(spread + 1e-05)


def position_index():
    token_slot = jnp.arange(WZ * WH * WW, dtype=jnp.int32)
    level_pos = token_slot // (WH * WW)
    lat_pos = token_slot // WW % WH
    lon_pos = token_slot % WW
    index = (level_pos[:, None] * WZ + level_pos[None, :]) * WH + lat_pos[:, None]
    index = (index * WH + lat_pos[None, :]) * (2 * WW - 1)
    return index + lon_pos[:, None] - lon_pos[None, :] + WW - 1


def group_labels(levels, rows, total_rows, band_start):
    token_slot = jnp.arange(WZ * WH * WW, dtype=jnp.int32)
    level_index = (
        jnp.arange(levels // WZ, dtype=jnp.int32)[:, None, None] * WZ
        + (token_slot // (WH * WW))[None, None, :]
    )
    lat_index = (
        band_start
        + jnp.arange(rows // WH, dtype=jnp.int32)[None, :, None] * WH
        + (token_slot // WW % WH)[None, None, :]
    )
    level_group = (level_index >= levels - WZ).astype(jnp.int32) + (
        level_index >= levels - WZ // 2
    ).astype(jnp.int32)
    lat_group = (lat_index >= total_rows - WH).astype(jnp.int32) + (
        lat_index >= total_rows - WH // 2
    ).astype(jnp.int32)
    return level_group * 3 + lat_group


def to_windows(stream):
    levels, rows, columns, width = stream.shape
    shaped = stream.reshape(levels // WZ, WZ, rows // WH, WH, columns // WW, WW, width)
    shaped = shaped.transpose(0, 2, 4, 1, 3, 5, 6)
    return shaped.reshape(levels // WZ, rows // WH, columns // WW, WZ * WH * WW, width)


def from_windows(windowed, levels, rows, columns):
    width = windowed.shape[-1]
    shaped = windowed.reshape(levels // WZ, rows // WH, columns // WW, WZ, WH, WW, width)
    return shaped.transpose(0, 3, 1, 4, 2, 5, 6).reshape(levels, rows, columns, width)


def attend_level(packed, offsets, labels):
    width = packed.shape[-1] // 3
    head_count = offsets.shape[1]
    head_size = width // head_count
    shape = packed.shape[:-1] + (head_count, head_size)
    queries = packed[..., :width].reshape(shape)
    keys_part = packed[..., width : 2 * width].reshape(shape)
    values_part = packed[..., 2 * width :].reshape(shape)
    scores = jnp.einsum(
        "abqhd,abkhd->abhqk", queries, keys_part, preferred_element_type=jnp.float32
    ) * head_size ** (-0.5)
    scores = scores + offsets.astype(jnp.float32)[:, None]
    same_group = labels[:, :, None] == labels[:, None, :]
    scores = jnp.where(same_group[:, None, None], scores, -jnp.inf)
    attention_weights = jax.nn.softmax(scores, axis=-1).astype(jnp.bfloat16)
    mixed = jnp.einsum(
        "abhqk,abkhd->abqhd", attention_weights, values_part, preferred_element_type=jnp.float32
    )
    return mixed.astype(jnp.bfloat16).reshape(packed.shape[:-1] + (width,))


def run_block(stream, w_qkv, w_proj, w_up, w_down, table_rows, labels):
    levels, rows, columns, width = stream.shape
    normed = layer_norm(stream).astype(jnp.bfloat16)
    packed = jnp.dot(normed.reshape(-1, width), w_qkv, preferred_element_type=jnp.float32).astype(
        jnp.bfloat16
    )
    windowed = to_windows(packed.reshape(levels, rows, columns, 3 * width))
    offsets = jnp.take(table_rows, position_index(), axis=-1)

    def per_level(inputs):
        return attend_level(inputs[0], inputs[1], inputs[2])

    attended = lax.map(per_level, (windowed, offsets, labels))
    attended = from_windows(attended, levels, rows, columns)
    projected = jnp.dot(
        attended.reshape(-1, width), w_proj, preferred_element_type=jnp.float32
    ).reshape(stream.shape)
    middle = (stream.astype(jnp.float32) + projected).astype(jnp.bfloat16)
    lifted_in = layer_norm(middle).astype(jnp.bfloat16).reshape(-1, width)
    raised = jnp.dot(lifted_in, w_up, preferred_element_type=jnp.float32)
    activated = jax.nn.gelu(raised, approximate=True).astype(jnp.bfloat16)
    lowered = jnp.dot(activated, w_down, preferred_element_type=jnp.float32).reshape(stream.shape)
    return (middle.astype(jnp.float32) + lowered).astype(jnp.bfloat16)


def advance_lat(stream):
    strip = stream[:, : WH // 2]
    arrived = passed_along(strip, "lat", -1)
    return jnp.concatenate([stream[:, WH // 2 :], arrived], axis=1)


def advance_lon(stream):
    strip = stream[:, :, : WW // 2]
    arrived = passed_along(strip, "lon", -1)
    return jnp.concatenate([stream[:, :, WW // 2 :], arrived], axis=2)


def return_lat(stream):
    strip = stream[:, stream.shape[1] - WH // 2 :]
    arrived = passed_along(strip, "lat", 1)
    return jnp.concatenate([arrived, stream[:, : stream.shape[1] - WH // 2]], axis=1)


def return_lon(stream):
    strip = stream[:, :, stream.shape[2] - WW // 2 :]
    arrived = passed_along(strip, "lon", 1)
    return jnp.concatenate([arrived, stream[:, :, : stream.shape[2] - WW // 2]], axis=2)


def pick_types(flat_table, type_index, types_all):
    picked = jnp.take(flat_table.reshape(-1, types_all), type_index, axis=1)
    return picked.reshape(-1)


def arrange_rows(picked_flat, level_windows):
    shaped = picked_flat.reshape(level_windows, HEADS, RELPOS, -1)
    return shaped.transpose(0, 3, 1, 2)


def body(
    tokens,
    surface_ids,
    surface_embed,
    type_index,
    bias_plain,
    bias_shift,
    w_qkv,
    w_proj,
    w_up,
    w_down,
):
    width = HEADS * HEAD_DIM
    levels, rows = (tokens.shape[0], tokens.shape[1])
    columns = tokens.shape[2] // width
    level_windows = levels // WZ
    grid = tokens.reshape(levels, rows, columns, width)
    qkv_all = w_qkv.reshape(2, width, 3 * width)
    proj_all = w_proj.reshape(2, width, width)
    down_all = w_down.reshape(2, 4 * width, width)
    types_all = bias_plain.shape[0] * lax.axis_size("lon") // (level_windows * HEADS * RELPOS)
    classes = jnp.arange(surface_embed.shape[0], dtype=jnp.int32)
    onehot = surface_ids[:, :, None] == classes
    added = jnp.sum(jnp.where(onehot[..., None], surface_embed.astype(jnp.float32), 0.0), axis=2)
    stream = (grid.astype(jnp.float32) + added[None]).astype(jnp.bfloat16)
    full_plain, full_shift = (
        lax.all_gather(bias_plain, "lon", axis=0, tiled=True),
        lax.all_gather(bias_shift, "lon", axis=0, tiled=True),
    )
    rows_plain = arrange_rows(pick_types(full_plain, type_index, types_all), level_windows)
    rows_shift = arrange_rows(pick_types(full_shift, type_index, types_all), level_windows)
    plain_labels = jnp.zeros((level_windows, rows // WH, WZ * WH * WW), jnp.int32)
    stream = run_block(
        stream, qkv_all[0], proj_all[0], w_up[0], down_all[0], rows_plain, plain_labels
    )
    stream = jnp.roll(stream, -(WZ // 2), axis=0)
    stream = advance_lon(advance_lat(stream))
    band = lax.axis_index("lat")
    labels = group_labels(levels, rows, rows * lax.axis_size("lat"), band * rows)
    stream = run_block(stream, qkv_all[1], proj_all[1], w_up[1], down_all[1], rows_shift, labels)
    stream = return_lat(return_lon(stream))
    stream = jnp.roll(stream, WZ // 2, axis=0)
    return stream.reshape(levels, rows, columns * width)


def solution(mesh):
    return jax.shard_map(
        body,
        mesh=mesh,
        in_specs=(
            P(None, "lat", "lon"),
            P("lat", "lon"),
            P(),
            P("lat"),
            P("lon"),
            P("lon"),
            P(),
            P(),
            P(),
            P(),
        ),
        out_specs=P(None, "lat", "lon"),
        check_vma=False,
    )
```

profile of v0, /device:TPU:0, one launch (start us, length us, event | category | flops | bytes accessed | tf_op | source)
XLA Modules:
  0.0 719.1 jit_solution(4898500842779872174)
XLA Ops:
  6.5 1.9 reshape.585
  8.5 1.8 reshape.587
  13.5 3.0 slice_reduce_fusion.2
  19.5 2.3 copy.97
  23.3 6.2 slice_reduce_fusion
  35.4 36.2 %all-gather.5.cloned.1.call-done = bf16[16,1,79488]{2,1,0:T(2,128)(2,1)} async-done(((bf16[1,1,79488]{2,1,0:T(2,128)(2,1)}), bf16[16,1,79488]{2,1,0:T(2,128)(2,1)}) %all-gather.5.cloned.1.call-update) | async-done | bytes 2543632 | tf_op jit(solution)/shard_map/all_gather | solution.py:176
  71.7 53.6 %reduce.9 = bf16[16,79488]{1,0:T(8,128)(2,1)S(1)} reduce(bf16[16,1,79488]{2,1,0:T(2,128)(2,1)} %all-gather.5.cloned.1.call-done, bf16[]{:T(256)} %constant.165), dimensions={1}, to_apply=%all-gather.reduce_sub_computation | reduce | bytes 5087234 | tf_op jit(solution)/shard_map/all_gather | solution.py:176
  125.2 22.2 %reshape.536 = bf16[79488,16]{1,0:T(8,128)(2,1)} reshape(bf16[16,79488]{1,0:T(8,128)(2,1)S(1)} %reduce.9) | data formatting | bytes 5087232 | tf_op jit(solution)/shard_map/reshape | solution.py:141
  147.4 15.1 %copy.98 = bf16[79488,16]{0,1:T(8,128)(2,1)S(1)} copy(bf16[79488,16]{1,0:T(8,128)(2,1)} %reshape.536) | data formatting | bytes 5087232 | tf_op jit(solution)/shard_map/reshape | solution.py:141
  162.6 55.1 %reduce.13 = bf16[16,79488]{1,0:T(8,128)(2,1)} reduce(bf16[16,1,79488]{2,1,0:T(2,128)(2,1)} %all-gather.7.cloned.1.call-done, bf16[]{:T(256)} %constant.165), dimensions={1}, to_apply=%all-gather.1.reduce_sub_computation | reduce | bytes 5087234 | tf_op jit(solution)/shard_map/all_gather | solution.py:177
  217.7 24.2 %reshape.540 = bf16[79488,16]{1,0:T(8,128)(2,1)} reshape(bf16[16,79488]{1,0:T(8,128)(2,1)} %reduce.13) | data formatting | bytes 5087232 | tf_op jit(solution)/shard_map/reshape | solution.py:141
  241.9 15.6 %copy.109 = bf16[79488,16]{0,1:T(8,128)(2,1)} copy(bf16[79488,16]{1,0:T(8,128)(2,1)} %reshape.540) | data formatting | bytes 5087232 | tf_op jit(solution)/shard_map/reshape | solution.py:141
  258.5 3.3 gather_fusion.2
  264.1 7.6 %copy.99 = bf16[4,6,3312,2]{1,0,2,3:T(4,128)(2,1)} copy(bf16[4,6,3312,2]{2,1,0,3:T(8,128)(2,1)S(1)} %reshape_reshape.15) | data formatting | bytes 635904 | tf_op jit(solution)/shard_map/reshape;reshape | solution.py:146
  271.6 70.8 %gather_fusion.1 = bf16[20736,4,2,6]{3,1,2,0:T(4,128)(2,1)} fusion(bf16[4,2,6,3312]{2,0,3,1:T(4,128)(2,1)} %bitcast.149, s32[21504]{0:T(1024)S(1)} %pad_clamp_fusion), kind=kCustom, calls=%fused_computation.1.clone | custom fusion | bytes 4064256 | tf_op jit(solution)/shard_map/jit(_take)/gather | solution.py:98
  342.4 70.1 %copy.125 = bf16[144,144,4,2,6]{1,0,3,4,2:T(8,128)(2,1)S(1)} copy(bf16[144,144,4,2,6]{4,2,3,1,0:T(4,128)(2,1)} %bitcast.147) | data formatting | bytes 3981312 | tf_op jit(solution)/shard_map/jit(_take)/gather | solution.py:98
  412.5 2.7 reshape_reshape.17
  415.2 8.9 %copy.110 = bf16[4,6,3312,2]{1,0,2,3:T(4,128)(2,1)} copy(bf16[4,6,3312,2]{2,1,0,3:T(8,128)(2,1)} %reshape_reshape.17) | data formatting | bytes 635904 | tf_op jit(solution)/shard_map/reshape;reshape | solution.py:146
  424.2 70.5 %gather_fusion.3 = bf16[20736,4,2,6]{3,1,2,0:T(4,128)(2,1)} fusion(bf16[4,2,6,3312]{2,0,3,1:T(4,128)(2,1)} %bitcast.148, s32[21504]{0:T(1024)} %copy-done.6), kind=kCustom, calls=%fused_computation.3.clone | custom fusion | bytes 4064256 | tf_op jit(solution)/shard_map/jit(_take)/gather | solution.py:98
  494.7 71.1 %copy.128 = bf16[144,144,4,2,6]{1,0,3,4,2:T(8,128)(2,1)} copy(bf16[144,144,4,2,6]{4,2,3,1,0:T(4,128)(2,1)} %bitcast.146) | data formatting | bytes 3981312 | tf_op jit(solution)/shard_map/jit(_take)/gather | solution.py:98
  565.8 5.4 select_bitcast_fusion
  572.3 35.3 %while.20 = (s32[]{:T(128)}, bf16[4,2,1,144,192]{4,1,3,0,2:T(2,128)(2,1)}, bf16[4,2,1,144,576]{4,1,3,0,2:T(2,128)(2,1)}, bf16[4,2,6,144,144]{4,3,1,2,0:T(8,128)(2,1)}, s32[]{:T(128)}) while((s32[]{:T(128)}, bf16[4,2,1,144,192]{4,1,3,0,2:T(2,128)(2,1)}, bf16[4,2,1,144,576]{4,1,3,0,2:T(2,128)(2,1)}, bf16[4,2,6,144,144]{4,3,1,2,0:T(8,128)(2,1)}, ...), condition=%wide.region_6.9_spmd, body=%wide.region_3.8_spmd.sunk | while | flops 33647760 | bytes 7405637 | solution.py:103
  576.6 2.0 fusion.98
  578.6 1.7 convolution_convert_fusion.6
  585.4 2.0 fusion.98
  587.4 1.7 convolution_convert_fusion.6
  594.1 2.0 fusion.98
  602.9 2.0 fusion.98
  604.9 1.7 convolution_convert_fusion.6
  610.9 2.5 fusion.23
  613.4 2.5 dot_general.48
  616.8 2.9 collective-permute-start
  619.8 4.5 collective-permute-done
  624.5 2.8 collective-permute-start.1
  627.3 5.3 collective-permute-done.1
  639.4 39.1 %while.21 = (s32[]{:T(128)}, bf16[4,2,1,144,192]{4,1,3,0,2:T(2,128)(2,1)}, bf16[4,2,1,144,576]{4,1,3,0,2:T(2,128)(2,1)S(1)}, s32[4,2,144]{2,1,0:T(2,128)S(1)}, bf16[4,2,6,144,144]{4,3,1,2,0:T(8,128)(2,1)}, /*index=5*/s32[]{:T(128)}) while((s32[]{:T(128)}, bf16[4,2,1,144,192]{4,1,3,0,2:T(2,128)(2,1)}, ...), condition=%wide.region_14.17_spmd, body=%wide.region_11.16_spmd.sunk | while | flops 33938064 | bytes 7492049 | solution.py:103
  643.4 3.1 fusion.103
  646.5 1.7 convolution_convert_fusion.7
  653.1 3.1 fusion.103
  656.3 1.7 convolution_convert_fusion.7
  662.9 3.1 fusion.103
  666.0 1.7 convolution_convert_fusion.7
  672.7 3.1 fusion.103
  675.8 1.7 convolution_convert_fusion.7
  683.1 2.5 fusion.22
  685.6 2.5 dot_general.54
  689.1 13.1 %collective-permute-done.2 = bf16[8,12,6,192]{3,2,1,0:T(8,128)(2,1)S(1)} collective-permute-done((bf16[8,12,6,192]{3,2,1,0:T(8,128)(2,1)S(1)}, bf16[8,12,6,192]{3,2,1,0:T(8,128)(2,1)S(1)}, u32[]{:S(2)}, u32[]{:S(2)}) %collective-permute-start.2) | collective-permute-done | bytes 221216 | tf_op jit(solution)/shard_map/ppermute | solution.py:17
  702.3 7.8 %collective-permute-done.3 = bf16[8,3,12,192]{3,2,1,0:T(8,128)(2,1)S(1)} collective-permute-done((bf16[8,3,12,192]{3,2,1,0:T(8,128)(2,1)S(1)}, bf16[8,3,12,192]{3,2,1,0:T(8,128)(2,1)S(1)}, u32[]{:S(2)}, u32[]{:S(2)}) %collective-permute-start.3) | collective-permute-done | bytes 110624 | tf_op jit(solution)/shard_map/ppermute | solution.py:17
  (191 shorter events, 77.7 us)
Async XLA Ops:
  6.5 4.1 copy-start.10
  6.5 65.1 %all-gather.5.cloned.1.call-start = ((), (), s32[]{:S(2)}) async-start(), calls=%async_computation | async-start | bytes 5405184 | tf_op jit(solution)/shard_map/all_gather | solution.py:176
  8.4 2.9 copy-start.18
  8.4 2.9 copy-start.17
  8.4 154.2 %all-gather.7.cloned.1.call-start = ((), (), s32[]{:S(2)}) async-start(), calls=%async_computation.1 | async-start | bytes 5405184 | tf_op jit(solution)/shard_map/all_gather | solution.py:177
  11.8 0.9 copy-start
  12.4 1.1 copy-start.5
  19.4 2.3 copy-start.9
  19.5 3.8 copy-start.4
  21.7 8.8 %copy-start.8 = (bf16[110592]{0:T(1024)(128)(2,1)S(1)}, bf16[110592]{0:T(1024)(128)(2,1)}, u32[]{:S(2)}) copy-start(bf16[110592]{0:T(1024)(128)(2,1)} %get-tuple-element.96) | copy-start | bytes 663556
  23.3 10.0 %copy-start.21 = (s32[2]{0:T(128)S(1)}, s32[2]{0:T(128)}, u32[]{:S(2)}) copy-start(s32[2]{0:T(128)} %param.21) | copy-start | bytes 28
  35.4 236.2 %copy-start.6 = (s32[21504]{0:T(1024)}, s32[21504]{0:T(1024)S(1)}, u32[]{:S(2)}) copy-start(s32[21504]{0:T(1024)S(1)} %pad_clamp_fusion) | copy-start | bytes 258052
  572.3 36.5 %copy-start.1 = (bf16[8,12,12,192]{3,2,1,0:T(8,128)(2,1)S(1)}, bf16[8,12,12,192]{3,2,1,0:T(8,128)(2,1)}, u32[]{:S(2)}) copy-start(bf16[8,12,12,192]{3,2,1,0:T(8,128)(2,1)} %copy-done) | copy-start | bytes 1327108
  572.3 36.5 %copy-start.11 = (bf16[192,192,1,1]{1,0,2,3:T(8,128)(2,1)S(1)}, bf16[192,192,1,1]{1,0,2,3:T(8,128)(2,1)}, u32[]{:S(2)}) copy-start(bf16[192,192,1,1]{1,0,2,3:T(8,128)(2,1)} %reshape.603) | copy-start | bytes 221188
  609.9 1.1 copy-start.19
  613.4 2.5 copy-start.13
  616.8 10.6 %copy-start.15 = (s32[4,144]{1,0:T(4,128)S(1)}, s32[4,144]{1,0:T(4,128)}, u32[]{:S(2)}) copy-start(s32[4,144]{1,0:T(4,128)} %add_multiply_fusion) | copy-start | bytes 6916
  616.8 10.6 %copy-start.16 = (s32[2,144]{1,0:T(2,128)S(1)}, s32[2,144]{1,0:T(2,128)}, u32[]{:S(2)}) copy-start(s32[2,144]{1,0:T(2,128)} %fusion.58) | copy-start | bytes 3460
  616.8 7.5 %collective-permute-start = (bf16[8,3,12,192]{3,2,1,0:T(8,128)(2,1)S(1)}, bf16[8,3,12,192]{3,2,1,0:T(8,128)(2,1)S(1)}, u32[]{:S(2)}, u32[]{:S(2)}) collective-permute-start(bf16[8,3,12,192]{3,2,1,0:T(8,128)(2,1)S(1)} %pad_maximum_fusion.7), channel_id=1, source_target_pairs={{16,0},{32,16},{48,32},{64,48},{80,64},{96,80},{112,96},{0,112},{1... | collective-permute-start | bytes 331784 | tf_op jit(solution)/shard_map/ppermute | solution.py:17
  624.5 9.3 %copy-start.2 = (bf16[8,12,6,192]{3,2,1,0:T(8,128)(2,1)}, bf16[8,12,6,192]{3,2,1,0:T(8,128)(2,1)S(1)}, u32[]{:S(2)}) copy-start(bf16[8,12,6,192]{3,2,1,0:T(8,128)(2,1)S(1)} %get-tuple-element.132) | copy-start | bytes 663556
  624.5 8.1 %collective-permute-start.1 = (bf16[8,12,6,192]{3,2,1,0:T(8,128)(2,1)S(1)}, bf16[8,12,6,192]{3,2,1,0:T(8,128)(2,1)S(1)}, u32[]{:S(2)}, u32[]{:S(2)}) collective-permute-start(bf16[8,12,6,192]{3,2,1,0:T(8,128)(2,1)S(1)} %get-tuple-element.133), channel_id=1, source_target_pairs={{1,0},{2,1},{3,2},{4,3},{5,4},{6,5},{7,6},{8,7},{9,8},{10,9},{11,1... | collective-permute-start | bytes 663560 | tf_op jit(solution)/shard_map/ppermute | solution.py:17
  632.6 1.2 copy-start.3
  633.8 0.9 copy-start.7
  639.4 40.3 %copy-start.14 = (bf16[192,192,1,1]{1,0,2,3:T(8,128)(2,1)S(1)}, bf16[192,192,1,1]{1,0,2,3:T(8,128)(2,1)}, u32[]{:S(2)}) copy-start(bf16[192,192,1,1]{1,0,2,3:T(8,128)(2,1)} %reshape.605) | copy-start | bytes 221188
  682.0 1.1 copy-start.20
  685.6 2.5 copy-start.12
  689.0 13.2 %collective-permute-start.2 = (bf16[8,12,6,192]{3,2,1,0:T(8,128)(2,1)S(1)}, bf16[8,12,6,192]{3,2,1,0:T(8,128)(2,1)S(1)}, u32[]{:S(2)}, u32[]{:S(2)}) collective-permute-start(bf16[8,12,6,192]{3,2,1,0:T(8,128)(2,1)S(1)} %get-tuple-element.130), channel_id=1, source_target_pairs={{15,0},{0,1},{1,2},{2,3},{3,4},{4,5},{5,6},{6,7},{7,8},{8,9},{9,10... | collective-permute-start | bytes 663560 | tf_op jit(solution)/shard_map/ppermute | solution.py:17
  702.2 7.8 %collective-permute-start.3 = (bf16[8,3,12,192]{3,2,1,0:T(8,128)(2,1)S(1)}, bf16[8,3,12,192]{3,2,1,0:T(8,128)(2,1)S(1)}, u32[]{:S(2)}, u32[]{:S(2)}) collective-permute-start(bf16[8,3,12,192]{3,2,1,0:T(8,128)(2,1)S(1)} %pad_maximum_fusion.6), channel_id=1, source_target_pairs={{112,0},{0,16},{16,32},{32,48},{48,64},{64,80},{80,96},{96,112},{1... | collective-permute-start | bytes 331784 | tf_op jit(solution)/shard_map/ppermute | solution.py:17
Sparse Core Ops, SparseCore 0:
  9.8 61.8 all-gather.4
  74.1 57.9 all-gather.6
where the time goes:
time: 729 us; the launch traced here: 719 us
  local copies, waits for them, and re-layouts  463 us (64%)
  other arithmetic  124 us (17%)
  waiting for transfers between devices  66.9 us (9%)
  matrix products  44.5 us (6%)
  between operations  14.3 us (2%)
    gather x4, local copies, waits for them, and re-layouts, run_block(): offsets = jnp.take(table_rows, position_index(), axis=-1)  282 us
    reshape x4, local copies, waits for them, and re-layouts, pick_types(): picked = jnp.take(flat_table.reshape(-1, types_all), type_index, axis=1)  77.1 us
    all_gather x1, other arithmetic, body(): lax.all_gather(bias_shift, 'lon', axis=0, tiled=True)  55.1 us
    all_gather x1, other arithmetic, body(): lax.all_gather(bias_plain, 'lon', axis=0, tiled=True)  53.6 us
    all_gather x1, waiting for transfers between devices, body(): lax.all_gather(bias_plain, 'lon', axis=0, tiled=True)  36.2 us
    ppermute x4, waiting for transfers between devices, passed_along(): return lax.ppermute(block, axis, route)  30.6 us
    dynamic_slice x32, local copies, waits for them, and re-layouts, run_block(): attended = lax.map(per_level, (windowed, offsets, labels))  27.9 us
    sub x8, matrix products, attend_level(): attention_weights = jax.nn.softmax(scores, axis=-1).astype(jnp.bfloat16)  20.7 us
  transfers between devices with their start and end apart: 6, of which 5 were waited for; matrix products, arithmetic and copies ran while one was open for 16% of the time, Pallas kernels for 0%

commit v1 on v0

v1 whole, which is shorter than its diff:
```python
import jax
import jax.numpy as jnp
import numpy as np
from jax import lax
from jax.experimental import pallas as pl
from jax.experimental.pallas import tpu as pltpu
from jax.sharding import PartitionSpec as P

HEADS = 6
HEAD_DIM = 32
C = 192
Z = 8
WZ = 2
WH = 6
WW = 12
ROWS = 12
COLS = 12
RELPOS = 3312
TYPES = 16
SPAN = 2 * WW - 1
STRIPS = 4
CELL = 144
TOKENS = 1152
HALF = 72
TABLES = 48
SHARD_ROWS = 36
KAPPA = WH * SPAN
LON = 16
BIG = 1e30
SCALE = HEAD_DIM**-0.5
PAIR = 2


def slot_positions():
    pos = np.arange(HALF)
    bh, ch, b3, c6 = pos // 36, pos // 18 % 2, pos // 6 % 3, pos % 6
    return bh * 3 + b3, ch * 6 + c6


def spread_matrix():
    b, c = slot_positions()
    out = np.zeros((2, 256, WW, 128), np.float32)
    for lane_type in range(2):
        for query_col in range(WW):
            row = b * SPAN + query_col - c + WW - 1 + lane_type * (KAPPA - 128)
            out[lane_type, row, query_col, np.arange(HALF)] = 1.0
    return out.reshape(2, 256, 6, 256).transpose(0, 2, 1, 3)


def query_tail():
    b, c = slot_positions()
    out = np.zeros((CELL, 256), np.float32)
    for a in range(2):
        rows = a * HALF + np.arange(HALF)
        out[rows, 32 + 16 * c + 8 * a + b] = 1.0
        out[rows, 224] = 1.0
        out[rows, 225 + a] = 1.0
        out[rows, 227 + b // 3] = 1.0
    return out


def mask_rows():
    b, _ = slot_positions()
    out = np.zeros((3, 32, 256), np.float32)
    for a in range(2):
        lanes = a * 128 + np.arange(HALF)
        out[0, 0, a * 128 + HALF : a * 128 + 128] = -BIG
        out[1, 1 + (1 - a), lanes] = -BIG
        out[2, 3 + (1 - b // 3), lanes] = -BIG
    return out


def head_lanes():
    out = np.zeros((HEADS, 1, C), np.float32)
    for head in range(HEADS):
        out[head, 0, head * HEAD_DIM : (head + 1) * HEAD_DIM] = 1.0
    return out


def normalised(x):
    center = jnp.sum(x, axis=-1, keepdims=True) * (1.0 / C)
    moved = x - center
    spread = jnp.sum(moved * moved, axis=-1, keepdims=True) * (1.0 / C)
    return moved * lax.rsqrt(spread + 1e-05)


def rounded(x):
    return x.astype(jnp.bfloat16).astype(jnp.float32)


def gelu(v):
    inner = v * (0.7978845608028654 + (0.7978845608028654 * 0.044715) * (v * v))
    return v * (0.5 + 0.5 * jnp.tanh(inner))


def dot(a, b):
    return jnp.dot(a, b, preferred_element_type=jnp.float32)


def dot_nt(a, b):
    return lax.dot_general(a, b, (((1,), (1,)), ((), ())), preferred_element_type=jnp.float32)


def take_strided(ref, start):
    near = ref[0, pl.ds(start, HALF, stride=8), :]
    far = ref[1, pl.ds(start, HALF, stride=8), :]
    return jnp.concatenate([near, far[:, : C - 128]], axis=1)


def put_strided(ref, start, value):
    blank = jnp.zeros((HALF, 256 - C), jnp.float32)
    ref[0, pl.ds(start, HALF, stride=8), :] = value[:, :128]
    ref[1, pl.ds(start, HALF, stride=8), :] = jnp.concatenate([value[:, 128:], blank], axis=1)


def take_rows(ref, start, count):
    return jnp.concatenate(
        [ref[0, pl.ds(start, count), :], ref[1, pl.ds(start, count), : C - 128]], axis=1
    )


def put_rows(ref, start, value):
    rows = pl.ds(start, value.shape[0])
    ref[0, rows, :] = value[:, :128]
    ref[1, rows, : C - 128] = value[:, 128:]


def spread_tables(block, gathered, spread, tables):
    for lane_type in range(2):
        left = gathered[block, :, :, 128 * lane_type : 128 * lane_type + 256].reshape(768, 256)

        def step(pair, carry):
            wide = dot(left, spread[lane_type, pair])
            wide = wide.reshape(24, 2, 2, 8, 256)
            for inner in range(2):
                for a in range(2):
                    part = wide[:, :, a, :, 128 * inner : 128 * inner + 128]
                    part = part.reshape(24, 16, 128).astype(jnp.bfloat16)
                    tables[
                        24 * lane_type : 24 * lane_type + 24,
                        2 * pair + inner,
                        :,
                        128 * a : 128 * a + 128,
                    ] = part
            return carry

        lax.fori_loop(0, 6, step, 0)


def run_block(block, x, y, tables, consts, weights, band):
    tail, masks, lanes = consts
    w_q, w_kt, w_v, w_proj, w_up, w_down = weights
    last_band = (band == lax.axis_size("lat") - 1).astype(jnp.float32) if block else None

    def step(pair, carry):
        lat_window = pair // 2
        starts, level_windows = [], []
        for i in range(PAIR):
            level_window = (pair % 2) * 2 + i
            level_windows.append(level_window)
            for a in range(2):
                level = lax.rem(2 * level_window + a + block, Z)
                starts.append(lat_window * (HALF * Z) + level)
        parts = [take_strided(x, s) for s in starts]
        stream = jnp.concatenate(parts, axis=0)
        normed = normalised(stream)
        normed_b = normed.astype(jnp.bfloat16)
        queries = dot(normed_b, w_q[block]) * SCALE
        blank = jnp.zeros((128 - HALF, C), jnp.float32)
        mixed_all = []
        for i in range(PAIR):
            first = normed[2 * i * HALF : (2 * i + 1) * HALF]
            second = normed[(2 * i + 1) * HALF : (2 * i + 2) * HALF]
            padded = jnp.concatenate([first, blank, second, blank], axis=0).astype(jnp.bfloat16)
            keys = dot_nt(w_kt[block], padded).astype(jnp.bfloat16)
            values = dot(padded, w_v[block]).astype(jnp.bfloat16)
            mask = masks[0]
            if block:
                on_level = (level_windows[i] == 3).astype(jnp.float32)
                on_lat = (lat_window == 1).astype(jnp.float32) * last_band
                mask = mask + masks[1] * on_level + masks[2] * on_lat
            mask = mask.astype(jnp.bfloat16)
            weight_parts, value_parts = [], []
            for head in range(HEADS):
                near = queries[i * CELL : (i + 1) * CELL, 128 * head : 128 * head + 128]
                near = (near + tail[:, 0:128]).astype(jnp.bfloat16)
                far = tail[:, 128:256].astype(jnp.bfloat16)
                left = jnp.concatenate([near, far], axis=1)
                table = tables[lat_window * 24 + level_windows[i] * HEADS + head].reshape(192, 256)
                right = jnp.concatenate([keys[32 * head : 32 * head + 32], table, mask], axis=0)
                scores = dot(left, right)
                top = jnp.max(scores, axis=-1, keepdims=True)
                grown = jnp.exp(scores - top)
                total = jnp.sum(grown, axis=-1, keepdims=True)
                weight_parts.append((grown * (1.0 / total)).astype(jnp.bfloat16))
                value_parts.append(values * lanes[head].astype(jnp.bfloat16))
            mixed_all.append(
                dot(jnp.concatenate(weight_parts, axis=1), jnp.concatenate(value_parts, axis=0))
            )
        mixed = jnp.concatenate(mixed_all, axis=0).astype(jnp.bfloat16)
        middle = rounded(stream + dot(mixed, w_proj[block]))
        lifted = gelu(dot(normalised(middle).astype(jnp.bfloat16), w_up[block]))
        result = middle + dot(lifted.astype(jnp.bfloat16), w_down[block])
        for j, s in enumerate(starts):
            put_strided(y, s, result[j * HALF : (j + 1) * HALF])
        return carry

    lax.fori_loop(0, 8 // PAIR, step, 0)


def kernel(
    tokens,
    ids,
    embed,
    picked,
    spread,
    tail,
    masks,
    lanes,
    w_q,
    w_kt,
    w_v,
    w_proj,
    w_up,
    w_down,
    out,
    gathered,
    tables,
    x,
    y,
    sent,
    received,
    back,
    returned,
    gather_send,
    gather_recv,
    halo_send,
    halo_recv,
):
    lat, lon = lax.axis_index("lat"), lax.axis_index("lon")
    lats, lons = lax.axis_size("lat"), lax.axis_size("lon")
    consts = (tail, masks, lanes)
    weights = (w_q, w_kt, w_v, w_proj, w_up, w_down)
    north, south = lax.rem(lat + lats - 1, lats), lax.rem(lat + 1, lats)
    west, east = lax.rem(lon + lons - 1, lons), lax.rem(lon + 1, lons)

    def place(i, j):
        return {"lat": i, "lon": j}

    barrier = pltpu.get_barrier_semaphore()
    for distance in range(1, LON):
        pl.semaphore_signal(
            barrier,
            inc=1,
            device_id=place(lat, lax.rem(lon + distance, lons)),
            device_id_type=pl.DeviceIdType.MESH,
        )
    for i, j in ((north, lon), (south, lon), (north, west), (south, east)):
        pl.semaphore_signal(
            barrier, inc=1, device_id=place(i, j), device_id_type=pl.DeviceIdType.MESH
        )
    pl.semaphore_wait(barrier, LON - 1 + 4)

    def share(block, distance, origin, target):
        return pltpu.make_async_remote_copy(
            src_ref=picked.at[block],
            dst_ref=gathered.at[block, origin],
            send_sem=gather_send.at[block, distance],
            recv_sem=gather_recv.at[block, distance],
            device_id=place(lat, target),
            device_id_type=pl.DeviceIdType.MESH,
        )

    for block in range(2):
        for distance in range(1, LON):
            share(block, distance, lon, lax.rem(lon + distance, lons)).start()
    for block in range(2):
        gathered[block, lon] = picked[block]

    def embed_row(row, carry):
        strip, inner = row // 3, row % 3
        for col in range(COLS):
            cell = tokens[row, :, C * col : C * col + C].astype(jnp.float32)
            line = embed[pl.ds(ids[row, col], 1), :]
            start = ((strip * 2 + col // 6) * 18 + inner * 6 + col % 6) * 8
            put_rows(x, pl.multiple_of(start, 8), rounded(cell + line))
        return carry

    lax.fori_loop(0, ROWS, embed_row, 0)

    def arrive(block):
        for distance in range(1, LON):
            share(block, distance, lax.rem(lon + lons - distance, lons), lon).wait_recv()

    arrive(0)
    spread_tables(0, gathered, spread, tables)
    run_block(0, x, y, tables, consts, weights, lat)

    for strip in range(STRIPS):
        for half in range(2):
            start = (strip * 2 + half) * CELL
            sent[strip, half] = take_rows(y, start, CELL).astype(jnp.bfloat16)

    def halo(index, source, target, i, j):
        return pltpu.make_async_remote_copy(
            src_ref=source,
            dst_ref=target,
            send_sem=halo_send.at[index],
            recv_sem=halo_recv.at[index],
            device_id=place(i, j),
            device_id_type=pl.DeviceIdType.MESH,
        )

    ahead = [
        halo(0, sent.at[1:4, 0], received.at[0:3], lat, west),
        halo(1, sent.at[0, 1], received.at[3], north, lon),
        halo(2, sent.at[0, 0], received.at[4], north, west),
    ]
    for copy in ahead:
        copy.start()
    arrive(1)
    spread_tables(1, gathered, spread, tables)
    for strip in range(3):
        start = strip * 2 * CELL
        put_rows(x, start, sent[strip + 1, 1].astype(jnp.float32))
    for copy in ahead:
        copy.wait()
    for strip in range(3):
        start = (strip * 2 + 1) * CELL
        put_rows(x, start, received[strip].astype(jnp.float32))
    put_rows(x, 6 * CELL, received[3].astype(jnp.float32))
    put_rows(x, 7 * CELL, received[4].astype(jnp.float32))
    run_block(1, x, y, tables, consts, weights, lat)

    for strip in range(STRIPS):
        for half in range(2):
            start = (strip * 2 + half) * CELL
            back[strip, half] = take_rows(y, start, CELL).astype(jnp.bfloat16)
    home = [
        halo(3, back.at[0:3, 1], returned.at[0:3], lat, east),
        halo(4, back.at[3, 0], returned.at[3], south, lon),
        halo(5, back.at[3, 1], returned.at[4], south, east),
    ]
    for copy in home:
        copy.start()
    for block in range(2):
        for distance in range(1, LON):
            share(block, distance, lon, lax.rem(lon + distance, lons)).wait_send()

    def put(strip, half, cells):
        for inner in range(3):
            for col in range(6):
                at = (inner * 6 + col) * 8
                lane = (half * 6 + col) * C
                out[strip * 3 + inner, :, lane : lane + C] = cells[at : at + 8].astype(jnp.bfloat16)

    for strip in range(3):
        put(strip + 1, 1, back[strip, 0].astype(jnp.float32))
    for copy in home:
        copy.wait()
    for strip in range(3):
        put(strip + 1, 0, returned[strip].astype(jnp.float32))
    put(0, 1, returned[3].astype(jnp.float32))
    put(0, 0, returned[4].astype(jnp.float32))


def pick_types(bias_plain, bias_shift, type_index):
    both = jnp.stack([bias_plain.reshape(SHARD_ROWS, -1), bias_shift.reshape(SHARD_ROWS, -1)])
    entry = jnp.arange(KAPPA * TYPES, dtype=jnp.int32)[:, None]
    lane = jnp.arange(384, dtype=jnp.int32)[None, :]
    wanted = jnp.where(lane < KAPPA, type_index[0], type_index[1])
    relative = jnp.where(lane < KAPPA, lane, lane - KAPPA)
    choose = (entry == relative * TYPES + wanted) & (lane < 2 * KAPPA)
    rows = jnp.dot(
        both.reshape(2 * SHARD_ROWS, -1),
        choose.astype(jnp.bfloat16),
        preferred_element_type=jnp.float32,
    ).astype(jnp.bfloat16)
    rows = rows.reshape(2, 6, 6, 384)
    return jnp.pad(rows, ((0, 0), (0, 0), (0, 2), (0, 0))).reshape(2, 48, 384)


def body(
    tokens,
    surface_ids,
    surface_embed,
    type_index,
    bias_plain,
    bias_shift,
    w_qkv,
    w_proj,
    w_up,
    w_down,
):
    picked = pick_types(bias_plain, bias_shift, type_index)
    qkv = w_qkv.reshape(2, C, 3 * C)
    w_q = jnp.pad(
        qkv[:, :, :C].reshape(2, C, HEADS, HEAD_DIM), ((0, 0), (0, 0), (0, 0), (0, 128 - HEAD_DIM))
    ).reshape(2, C, HEADS * 128)
    w_kt = qkv[:, :, C : 2 * C].transpose(0, 2, 1)
    w_v = qkv[:, :, 2 * C :]
    spread = jnp.asarray(spread_matrix(), jnp.bfloat16)
    tail = jnp.asarray(query_tail(), jnp.float32)
    masks = jnp.asarray(mask_rows(), jnp.float32)
    lanes = jnp.asarray(head_lanes(), jnp.float32)
    in_vmem = pl.BlockSpec(memory_space=pltpu.VMEM)
    rows = pl.pallas_call(
        kernel,
        out_shape=jax.ShapeDtypeStruct((ROWS, Z, COLS * C), jnp.bfloat16),
        in_specs=[in_vmem, pl.BlockSpec(memory_space=pltpu.SMEM)] + [in_vmem] * 12,
        out_specs=in_vmem,
        scratch_shapes=[
            pltpu.VMEM((2, LON, 48, 384), jnp.bfloat16),
            pltpu.VMEM((TABLES, WW, 16, 256), jnp.bfloat16),
            pltpu.VMEM((2, TOKENS, 128), jnp.float32),
            pltpu.VMEM((2, TOKENS, 128), jnp.float32),
            pltpu.VMEM((STRIPS, 2, CELL, C), jnp.bfloat16),
            pltpu.VMEM((5, CELL, C), jnp.bfloat16),
            pltpu.VMEM((STRIPS, 2, CELL, C), jnp.bfloat16),
            pltpu.VMEM((5, CELL, C), jnp.bfloat16),
            pltpu.SemaphoreType.DMA((2, LON)),
            pltpu.SemaphoreType.DMA((2, LON)),
            pltpu.SemaphoreType.DMA((6,)),
            pltpu.SemaphoreType.DMA((6,)),
        ],
        compiler_params=pltpu.CompilerParams(
            collective_id=0, has_side_effects=True, vmem_limit_bytes=56 * 1024 * 1024
        ),
    )(
        tokens.transpose(1, 0, 2),
        surface_ids,
        surface_embed.astype(jnp.float32),
        picked,
        spread,
        tail,
        masks,
        lanes,
        w_q,
        w_kt,
        w_v,
        w_proj.reshape(2, C, C),
        w_up,
        w_down.reshape(2, 4 * C, C),
    )
    return rows.transpose(1, 0, 2)


def solution(mesh):
    return jax.shard_map(
        body,
        mesh=mesh,
        in_specs=(
            P(None, "lat", "lon"),
            P("lat", "lon"),
            P(),
            P("lat"),
            P("lon"),
            P("lon"),
            P(),
            P(),
            P(),
            P(),
        ),
        out_specs=P(None, "lat", "lon"),
        check_vma=False,
    )
```

time: 729 us -> 77.6 us (0.11); the launches traced: 719 us -> 77.4 us
  local copies, waits for them, and re-layouts: 463 us -> 12.3 us
  other arithmetic: 124 us -> 2.59 us
  waiting for transfers between devices: 66.9 us -> 0 us
  Pallas kernels: 0 us -> 61.5 us
  matrix products: 44.5 us -> 0.86 us
  between operations: 14.3 us -> 0.09 us
    gather x6 -> x0, local copies, waits for them, and re-layouts: 287 us -> none  [the longest x4 282 us: run_block(): offsets = jnp.take(table_rows, position_index(), axis=-1)]
    all_gather x2 -> x0, other arithmetic: 109 us -> none  [the longest x1 55.1 us: body(): lax.all_gather(bias_shift, 'lon', axis=0, tiled=True)]
    reshape x8 -> x7, local copies, waits for them, and re-layouts: 79.3 us -> 5.02 us  [the longest x1 1.77 us: body(): w_down.reshape(2, 4 * C, C)]
    pallas_call x0 -> x1, Pallas kernels: none -> 61.5 us  [body(): pl.pallas_call(kernel, out_shape=jax.ShapeDtypeStruct((ROWS, Z, COLS * C)...]
    all_gather x2 -> x0, waiting for transfers between devices: 36.3 us -> none  [the longest x1 36.2 us: body(): lax.all_gather(bias_plain, 'lon', axis=0, tiled=True)]
    ppermute x4 -> x0, waiting for transfers between devices: 30.6 us -> none  [passed_along(): return lax.ppermute(block, axis, route)]
    dynamic_slice x32 -> x0, local copies, waits for them, and re-layouts: 27.9 us -> none  [run_block(): attended = lax.map(per_level, (windowed, offsets, labels))]
    dot_general x16 -> x1, matrix products: 23.8 us -> 0.86 us  [pick_types(): jnp.dot(both.reshape(2 * SHARD_ROWS, -1), choose.astype(jnp.bfloat16), pr...]
  transfers between devices with their start and end apart: 6 -> 0, of which waited for: 5 -> 0; matrix products, arithmetic and copies ran while one was open for 16% -> 0% of each run, Pallas kernels for 0% -> 0%
where the time goes in v1:
time: 77.6 us; the launch traced here: 77.4 us
  Pallas kernels  61.5 us (79%)
  local copies, waits for them, and re-layouts  12.3 us (16%)
  other arithmetic  2.59 us (3%)
  matrix products  0.86 us (1%)
    pallas_call x1, Pallas kernels, body(): pl.pallas_call(kernel, out_shape=jax.ShapeDtypeStruct((ROWS, Z, COLS * C)...  61.5 us
    another operation x2, local copies, waits for them, and re-layouts, pick_types(): jnp.stack([bias_plain.reshape(SHARD_ROWS, -1), bias_shift.reshape(SHARD_R...  2.37 us
    unnamed x7, local copies, waits for them, and re-layouts  1.82 us
    reshape x1, local copies, waits for them, and re-layouts, body(): w_down.reshape(2, 4 * C, C)  1.77 us

profile of v1, /device:TPU:0, one launch (start us, length us, event | category | flops | bytes accessed | tf_op | source)
XLA Modules:
  0.0 77.4 jit_solution(14362605128254844710)
XLA Ops:
  0.0 1.3 %fusion.12 = (s32[1]{0:T(128)}, s32[1]{0:T(128)}) fusion(s32[2]{0:T(128)} %param.17), kind=kLoop, calls=%fused_computation.17 | loop fusion | bytes 16 | tf_op jit(solution)/shard_map/slice | solution.py:371
  1.3 1.3 %fusion.9 = s32[384]{0:T(512)S(1)} fusion(s32[]{:T(128)} %bitcast.2, s32[]{:T(128)} %bitcast.1), kind=kLoop, calls=%fused_computation.13 | loop fusion | flops 2304 | bytes 1544 | tf_op jit(solution)/shard_map/add | solution.py:373
  2.6 1.3 %convert_element_type.11.embed = f32[3,192]{1,0:T(4,128)} convert(bf16[3,192]{1,0:T(4,128)(2,1)} %param.16) | non-fusion elementwise | flops 576 | bytes 3456 | tf_op jit(solution)/shard_map/convert_element_type | solution.py:432
  3.9 1.2 %stack_reshape.6 = bf16[1,36,2208]{2,1,0:T(8,128)(2,1)S(1)} reshape(bf16[79488]{0:T(1024)(128)(2,1)} %param.18) | data formatting | bytes 317952 | tf_op jit(solution)/shard_map/stack;reshape | solution.py:368
  5.1 1.2 %stack_reshape.7 = bf16[1,36,2208]{2,1,0:T(8,128)(2,1)S(1)} reshape(bf16[79488]{0:T(1024)(128)(2,1)} %param.19) | data formatting | bytes 317952 | tf_op jit(solution)/shard_map/stack;reshape | solution.py:368
  6.3 0.0 copy-start.2
  6.3 0.1 reshape.48
  6.4 0.0 copy-start.1
  6.4 0.9 %fusion.5 = bf16[72,384]{1,0:T(8,128)(2,1)S(1)} fusion(bf16[72,2208]{1,0:T(8,128)(2,1)S(1)} %reshape.48, s32[384]{0:T(512)S(1)} %fusion.9, pred[384]{0:T(512)(128)(4,1)S(1)} %iota_compare_fusion.2), kind=kOutput, calls=%fused_computation.5 | convolution fusion | flops 123816960 | bytes 375168 | tf_op jit(solution)/shard_map/dot_general | solution.py:374
  7.3 0.6 pad_bitcast_fusion.picked
  8.0 0.0 copy-done.2
  8.0 0.9 %reshape.54.w_proj = bf16[2,192,192]{2,1,0:T(8,128)(2,1)} reshape(bf16[2,36864]{1,0:T(2,128)(2,1)S(1)} %copy-done.2) | data formatting | bytes 294912 | tf_op jit(solution)/shard_map/reshape | solution.py:441
  8.9 0.0 copy-done.1
  8.9 0.5 reshape.51
  9.4 0.8 fusion.11
  10.1 0.0 copy-start
  10.1 0.8 %copy.18.w_kt = bf16[2,192,192]{2,1,0:T(8,128)(2,1)} copy(bf16[2,192,192]{1,2,0:T(8,128)(2,1)S(1)} %get-tuple-element.6) | data formatting | bytes 294912 | tf_op jit(solution)/shard_map/transpose | solution.py:400
  11.0 0.1 copy.16
  11.1 0.1 pad.9
  11.2 1.1 %copy.19.w_q = bf16[2,192,768]{2,1,0:T(8,128)(2,1)} copy(bf16[2,192,768]{1,2,0:T(8,128)(2,1)S(1)} %bitcast.11) | data formatting | bytes 1179648 | tf_op jit(solution)/shard_map/reshape | solution.py:399
  12.3 0.0 copy-done
  12.3 1.8 %reshape.55.w_down = bf16[2,768,192]{2,1,0:T(8,128)(2,1)} reshape(bf16[2,147456]{1,0:T(2,128)(2,1)S(1)} %copy-done) | data formatting | bytes 1179648 | tf_op jit(solution)/shard_map/reshape | solution.py:443
  14.0 61.5 %shard_map.136 = bf16[12,8,2304]{2,1,0:T(8,128)(2,1)} custom-call(bf16[12,8,2304]{2,1,0:T(8,128)(2,1)} %bitcast.14, s32[12,12]{1,0:T(8,128)} %ids.1, f32[3,192]{1,0:T(4,128)} %convert_element_type.11.embed, bf16[2,48,384]{2,1,0:T(8,128)(2,1)} %pad_bitcast_fusion.picked, bf16[2,6,256,256]{3,2,1,0:T(8,128)(2,1)} %constant.19.clone.spread, ...), custom_call_target="tpu_custom_call" | custom-call | tf_op jit(solution)/shard_map/pallas_call | solution.py:407
  75.5 1.8 %copy.21 = bf16[8,12,2304]{2,0,1:T(8,128)(2,1)} copy(bf16[8,12,2304]{2,0,1:T(8,128)(2,1)} %bitcast.12) | data formatting | bytes 884736
  (3 shorter events, 0.1 us)
Async XLA Ops:
  6.3 1.7 %copy-start.2 = (bf16[2,36864]{1,0:T(2,128)(2,1)S(1)}, bf16[2,36864]{1,0:T(2,128)(2,1)}, u32[]{:S(2)}) copy-start(bf16[2,36864]{1,0:T(2,128)(2,1)} %param.21) | copy-start | bytes 442372
  6.4 2.5 %copy-start.1 = (bf16[2,110592]{1,0:T(2,128)(2,1)S(1)}, bf16[2,110592]{1,0:T(2,128)(2,1)}, u32[]{:S(2)}) copy-start(bf16[2,110592]{1,0:T(2,128)(2,1)} %param.20) | copy-start | bytes 1327108
  10.1 2.1 %copy-start = (bf16[2,147456]{1,0:T(2,128)(2,1)S(1)}, bf16[2,147456]{1,0:T(2,128)(2,1)}, u32[]{:S(2)}) copy-start(bf16[2,147456]{1,0:T(2,128)(2,1)} %param.23) | copy-start | bytes 1769476

commit v2 on v1

v2 whole, which is shorter than its diff:
```python
import jax
import jax.numpy as jnp
import numpy as np
from jax import lax
from jax.experimental import pallas as pl
from jax.experimental.pallas import tpu as pltpu
from jax.sharding import PartitionSpec as P

HEADS = 6
HEAD_DIM = 32
C = 192
Z = 8
WZ = 2
WH = 6
WW = 12
ROWS = 12
COLS = 12
RELPOS = 3312
TYPES = 16
SPAN = 2 * WW - 1
STRIPS = 4
CELL = 144
TOKENS = 1152
HALF = 72
TABLES = 48
SHARD_LINES = 621
STRIDE = 69
CHUNKS = 18
KAPPA = WH * SPAN
LON = 16
BIG = 1e30
SCALE = HEAD_DIM**-0.5
PAIR = 2


def slot_positions():
    pos = np.arange(HALF)
    bh, ch, b3, c6 = pos // 36, pos // 18 % 2, pos // 6 % 3, pos % 6
    return bh * 3 + b3, ch * 6 + c6


def spread_matrix():
    b, c = slot_positions()
    out = np.zeros((2, 256, WW, 128), np.float32)
    for lane_type in range(2):
        for query_col in range(WW):
            row = b * SPAN + query_col - c + WW - 1 + lane_type * (KAPPA - 128)
            out[lane_type, row, query_col, np.arange(HALF)] = 1.0
    return out.reshape(2, 256, 6, 256).transpose(0, 2, 1, 3)


def query_tail():
    b, c = slot_positions()
    out = np.zeros((CELL, 256), np.float32)
    for a in range(2):
        rows = a * HALF + np.arange(HALF)
        out[rows, 32 + 16 * c + 8 * a + b] = 1.0
        out[rows, 224] = 1.0
        out[rows, 225 + a] = 1.0
        out[rows, 227 + b // 3] = 1.0
    return out


def mask_rows():
    b, _ = slot_positions()
    out = np.zeros((3, 32, 256), np.float32)
    for a in range(2):
        lanes = a * 128 + np.arange(HALF)
        out[0, 0, a * 128 + HALF : a * 128 + 128] = -BIG
        out[1, 1 + (1 - a), lanes] = -BIG
        out[2, 3 + (1 - b // 3), lanes] = -BIG
    return out


def head_lanes():
    out = np.zeros((HEADS, 1, C), np.float32)
    for head in range(HEADS):
        out[head, 0, head * HEAD_DIM : (head + 1) * HEAD_DIM] = 1.0
    return out


def normalised(x):
    center = jnp.sum(x, axis=-1, keepdims=True) * (1.0 / C)
    moved = x - center
    spread = jnp.sum(moved * moved, axis=-1, keepdims=True) * (1.0 / C)
    return moved * lax.rsqrt(spread + 1e-05)


def rounded(x):
    return x.astype(jnp.bfloat16).astype(jnp.float32)


def gelu(v):
    inner = v * (0.7978845608028654 + (0.7978845608028654 * 0.044715) * (v * v))
    return v * (0.5 + 0.5 * jnp.tanh(inner))


def dot(a, b):
    return jnp.dot(a, b, preferred_element_type=jnp.float32)


def dot_nt(a, b):
    return lax.dot_general(a, b, (((1,), (1,)), ((), ())), preferred_element_type=jnp.float32)


def take_strided(ref, start):
    near = ref[0, pl.ds(start, HALF, stride=8), :]
    far = ref[1, pl.ds(start, HALF, stride=8), :]
    return jnp.concatenate([near, far[:, : C - 128]], axis=1)


def put_strided(ref, start, value):
    blank = jnp.zeros((HALF, 256 - C), jnp.float32)
    ref[0, pl.ds(start, HALF, stride=8), :] = value[:, :128]
    ref[1, pl.ds(start, HALF, stride=8), :] = jnp.concatenate([value[:, 128:], blank], axis=1)


def take_rows(ref, start, count):
    return jnp.concatenate(
        [ref[0, pl.ds(start, count), :], ref[1, pl.ds(start, count), : C - 128]], axis=1
    )


def put_rows(ref, start, value):
    rows = pl.ds(start, value.shape[0])
    ref[0, rows, :] = value[:, :128]
    ref[1, rows, : C - 128] = value[:, 128:]


def pick_types(block, lines, types, choose, ordered, picked):
    lane = lax.broadcasted_iota(jnp.int32, (1, 384), 1)
    second = lane >= KAPPA
    kappa = jnp.where(second, lane - KAPPA, lane)
    for phase in range(4):
        group = jnp.where(lane < 2 * KAPPA, (kappa + 2 * phase) // 8, -1)
        left = jnp.concatenate(
            [
                lines[block, pl.ds(17 * phase + chunk, 16, stride=STRIDE), :]
                for chunk in range(CHUNKS)
            ],
            axis=0,
        ).astype(jnp.bfloat16)
        wide = dot(left, choose[phase])
        total = jnp.zeros((16, 384), jnp.float32)
        for chunk in range(CHUNKS):
            total = jnp.where(group == chunk, wide[16 * chunk : 16 * chunk + 16], total)
        for tile in range(3):
            ordered[tile, pl.ds(phase, 16, stride=4), :] = total[:, 128 * tile : 128 * tile + 128]
    row = lax.broadcasted_iota(jnp.int32, (8, 384), 0)
    groups = []
    for group in range(6):
        whole = jnp.concatenate([ordered[tile, 6 * group : 6 * group + 8, :] for tile in range(3)], axis=1)
        groups.append(jnp.where(row < 6, whole, 0.0))
    picked[block] = jnp.concatenate(groups, axis=0).astype(jnp.bfloat16)


def choose_lanes(types, choose):
    lane = lax.broadcasted_iota(jnp.int32, (1, 384), 1)
    second = lane >= KAPPA
    kappa = jnp.where(second, lane - KAPPA, lane)
    wanted = jnp.where(second, types[1], types[0])
    row = lax.broadcasted_iota(jnp.int32, (128, 384), 0)
    for phase in range(4):
        target = lax.rem(kappa + 2 * phase, 8) * TYPES + wanted
        target = jnp.where(lane < 2 * KAPPA, target, -1)
        choose[phase] = (row == target).astype(jnp.float32).astype(jnp.bfloat16)


def prepare_weights(qkv, w_q, w_kt):
    lane = lax.broadcasted_iota(jnp.int32, (1, HEADS * 128), 1)
    inner = lax.rem(lane, 128)
    target = jnp.where(inner < HEAD_DIM, (lane // 128) * HEAD_DIM + inner, -1)
    row = lax.broadcasted_iota(jnp.int32, (C, HEADS * 128), 0)
    place = (row == target).astype(jnp.float32).astype(jnp.bfloat16)
    one = lax.broadcasted_iota(jnp.int32, (C, C), 0) == lax.broadcasted_iota(jnp.int32, (C, C), 1)
    one = one.astype(jnp.float32).astype(jnp.bfloat16)
    for block in range(2):
        w_q[block] = dot(qkv[block, :, 0:C], place).astype(jnp.bfloat16)
        w_kt[block] = dot_nt(one, qkv[block, :, C : 2 * C]).astype(jnp.bfloat16)


def spread_tables(block, gathered, spread, tables):
    for lane_type in range(2):
        lanes = slice(128 * lane_type, 128 * lane_type + 256)
        left = jnp.concatenate(
            [
                gathered[block, c, x_of, z_of, :, lanes]
                for z_of in range(2)
                for x_of in range(4)
                for c in range(2)
            ],
            axis=0,
        )

        def step(pair, carry):
            wide = dot(left, spread[lane_type, pair])
            wide = wide.reshape(24, 2, 2, 8, 256)
            for inner in range(2):
                for a in range(2):
                    part = wide[:, :, a, :, 128 * inner : 128 * inner + 128]
                    part = part.reshape(24, 16, 128).astype(jnp.bfloat16)
                    tables[
                        24 * lane_type : 24 * lane_type + 24,
                        2 * pair + inner,
                        :,
                        128 * a : 128 * a + 128,
                    ] = part
            return carry

        lax.fori_loop(0, 6, step, 0)


def run_windows(block, lat_window, pair, x, y, tables, consts, weights, band):
    tail, masks, lanes = consts
    w_q, w_kt, w_v, w_proj, w_up, w_down = weights
    last_band = (band == lax.axis_size("lat") - 1).astype(jnp.float32)
    shifted = block.astype(jnp.float32)
    starts, level_windows = [], []
    for i in range(PAIR):
        level_window = pair * PAIR + i
        level_windows.append(level_window)
        for a in range(2):
            level = lax.rem(2 * level_window + a + block, Z)
            starts.append(lat_window * (HALF * Z) + level)
    parts = [take_strided(x, s) for s in starts]
    stream = jnp.concatenate(parts, axis=0)
    normed = normalised(stream)
    normed_b = normed.astype(jnp.bfloat16)
    queries = dot(normed_b, w_q[block]) * SCALE
    blank = jnp.zeros((128 - HALF, C), jnp.float32)
    mixed_all = []
    for i in range(PAIR):
        first = normed[2 * i * HALF : (2 * i + 1) * HALF]
        second = normed[(2 * i + 1) * HALF : (2 * i + 2) * HALF]
        padded = jnp.concatenate([first, blank, second, blank], axis=0).astype(jnp.bfloat16)
        keys = dot_nt(w_kt[block], padded).astype(jnp.bfloat16)
        values = dot(padded, w_v[block, :, 2 * C : 3 * C]).astype(jnp.bfloat16)
        on_level = (level_windows[i] == 3).astype(jnp.float32) * shifted
        on_lat = (lat_window == 1).astype(jnp.float32) * last_band * shifted
        mask = masks[0] + masks[1] * on_level + masks[2] * on_lat
        mask = mask.astype(jnp.bfloat16)
        weight_parts, value_parts = [], []
        for head in range(HEADS):
            near = queries[i * CELL : (i + 1) * CELL, 128 * head : 128 * head + 128]
            near = (near + tail[:, 0:128]).astype(jnp.bfloat16)
            far = tail[:, 128:256].astype(jnp.bfloat16)
            left = jnp.concatenate([near, far], axis=1)
            table = tables[lat_window * 24 + level_windows[i] * HEADS + head].reshape(192, 256)
            right = jnp.concatenate([keys[32 * head : 32 * head + 32], table, mask], axis=0)
            scores = dot(left, right)
            top = jnp.max(scores, axis=-1, keepdims=True)
            grown = jnp.exp(scores - top)
            total = jnp.sum(grown, axis=-1, keepdims=True)
            weight_parts.append((grown * (1.0 / total)).astype(jnp.bfloat16))
            value_parts.append(values * lanes[head].astype(jnp.bfloat16))
        mixed_all.append(
            dot(jnp.concatenate(weight_parts, axis=1), jnp.concatenate(value_parts, axis=0))
        )
    mixed = jnp.concatenate(mixed_all, axis=0).astype(jnp.bfloat16)
    middle = rounded(stream + dot(mixed, w_proj[block]))
    lifted = gelu(dot(normalised(middle).astype(jnp.bfloat16), w_up[block]))
    result = middle + dot(lifted.astype(jnp.bfloat16), w_down[block])
    for j, s in enumerate(starts):
        put_strided(y, s, result[j * HALF : (j + 1) * HALF])


def kernel(
    tokens_hbm,
    ids,
    types,
    embed_in,
    bias_plain,
    bias_shift,
    spread_hbm,
    tail,
    masks,
    lanes,
    qkv_hbm,
    proj_hbm,
    up_hbm,
    down_hbm,
    out,
    tokens,
    embed,
    lines,
    choose,
    ordered,
    picked,
    spread,
    qkv,
    w_q,
    w_kt,
    w_proj,
    w_up,
    w_down,
    gathered,
    tables,
    x,
    y,
    sent,
    received,
    back,
    returned,
    local_sems,
    gather_send,
    gather_recv,
    halo_send,
    halo_recv,
):
    lat, lon = lax.axis_index("lat"), lax.axis_index("lon")
    lats, lons = lax.axis_size("lat"), lax.axis_size("lon")
    consts = (tail, masks, lanes)
    weights = (w_q, w_kt, qkv, w_proj, w_up, w_down)
    north, south = lax.rem(lat + lats - 1, lats), lax.rem(lat + 1, lats)
    west, east = lax.rem(lon + lons - 1, lons), lax.rem(lon + 1, lons)

    sources = (tokens_hbm, qkv_hbm, spread_hbm, proj_hbm, up_hbm, down_hbm)
    targets = (tokens, qkv, spread, w_proj, w_up, w_down)
    loads = [
        pltpu.make_async_copy(source, target, local_sems.at[i])
        for i, (source, target) in enumerate(zip(sources, targets))
    ]
    for load in loads:
        load.start()

    def place(i, j):
        return {"lat": i, "lon": j}

    crosses, sides = 2, 2
    across = lons // (crosses * sides)
    core, x_at, z_at = lax.rem(lon, sides), lax.rem(lon // sides, across), lon // (sides * across)

    def lon_of(z, x, c):
        return (z * across + x) * sides + c

    opposite = lon_of(1 - z_at, x_at, core)
    sibling = lon_of(z_at, x_at, 1 - core)
    peers = [lon_of(z_at, lax.rem(x_at + step, across), core) for step in range(1, 4)]
    origins = [lax.rem(x_at + across - step, across) for step in range(1, 4)]
    partners = [(lat, j) for j in (opposite, sibling, *peers, west, east)]
    partners += [(north, lon), (south, lon), (north, west), (south, east)]

    barrier = pltpu.get_barrier_semaphore()
    for i, j in partners:
        pl.semaphore_signal(
            barrier, inc=1, device_id=place(i, j), device_id_type=pl.DeviceIdType.MESH
        )

    def share(block, index, source, slot, target):
        return pltpu.make_async_remote_copy(
            src_ref=source,
            dst_ref=slot,
            send_sem=gather_send.at[block, index],
            recv_sem=gather_recv.at[block, index],
            device_id=place(lat, target),
            device_id_type=pl.DeviceIdType.MESH,
        )

    def slot(block, x_of, z_of):
        return gathered.at[block, core, x_of, z_of]

    def own_copy(block, i):
        target = opposite if i == 0 else peers[i - 1]
        return share(block, i, picked.at[block], slot(block, x_at, z_at), target)

    def passed_copy(block, i):
        held = slot(block, x_at, 1 - z_at)
        return share(block, 4 + i, held, held, peers[i])

    def sibling_copy(block):
        held = gathered.at[block, core]
        return share(block, 7, held, held, sibling)

    def wait_opposite(block):
        share(block, 0, picked.at[block], slot(block, x_at, 1 - z_at), opposite).wait_recv()

    def wait_peers(block):
        for i, origin in enumerate(origins):
            share(block, 1 + i, picked.at[block], slot(block, origin, z_at), lon).wait_recv()
        for i, origin in enumerate(origins):
            share(block, 4 + i, picked.at[block], slot(block, origin, 1 - z_at), lon).wait_recv()

    def wait_sibling(block):
        other = gathered.at[block, 1 - core]
        share(block, 7, other, other, sibling).wait_recv()

    lines[0, 0:SHARD_LINES] = bias_plain[...].astype(jnp.float32)
    lines[1, 0:SHARD_LINES] = bias_shift[...].astype(jnp.float32)
    choose_lanes(types, choose)
    pl.semaphore_wait(barrier, len(partners))

    def pick_and_send(block, carry):
        pick_types(block, lines, types, choose, ordered, picked)
        for i in range(4):
            own_copy(block, i).start()
        gathered[block, core, x_at, z_at] = picked[block]
        return carry

    lax.fori_loop(0, 2, pick_and_send, 0)

    embed[0:3, :] = embed_in[...].astype(jnp.float32)
    loads[0].wait()

    def embed_row(row, carry):
        strip, inner = row // 3, row % 3
        for col in range(COLS):
            cell = tokens[row, :, C * col : C * col + C].astype(jnp.float32)
            line = embed[pl.ds(ids[row, col], 1), :]
            start = ((strip * 2 + col // 6) * 18 + inner * 6 + col % 6) * 8
            put_rows(x, pl.multiple_of(start, 8), rounded(cell + line))
        return carry

    lax.fori_loop(0, ROWS, embed_row, 0)

    def pass_on(block):
        wait_opposite(block)
        for i in range(3):
            passed_copy(block, i).start()

    pass_on(0)
    loads[1].wait()
    prepare_weights(qkv, w_q, w_kt)
    pass_on(1)
    wait_peers(0)
    sibling_copy(0).start()
    for load in loads[2:]:
        load.wait()

    def halo(index, source, target, i, j):
        return pltpu.make_async_remote_copy(
            src_ref=source,
            dst_ref=target,
            send_sem=halo_send.at[index],
            recv_sem=halo_recv.at[index],
            device_id=place(i, j),
            device_id_type=pl.DeviceIdType.MESH,
        )

    ahead = [
        halo(0, sent.at[0, 0], received.at[4], north, west),
        halo(1, sent.at[0, 1], received.at[3], north, lon),
        halo(2, sent.at[1, 0], received.at[0], lat, west),
        halo(3, sent.at[3, 0], received.at[2], lat, west),
        halo(4, sent.at[2, 0], received.at[1], lat, west),
    ]
    home = [
        halo(5, back.at[3, 1], returned.at[4], south, east),
        halo(6, back.at[3, 0], returned.at[3], south, lon),
        halo(7, back.at[2, 1], returned.at[2], lat, east),
        halo(8, back.at[0:2, 1], returned.at[0:2], lat, east),
    ]

    def narrow(target, strips):
        for strip in strips:
            for half in range(2):
                start = (strip * 2 + half) * CELL
                target[strip, half] = take_rows(y, start, CELL).astype(jnp.bfloat16)

    def widen(strip, half, source):
        put_rows(x, (strip * 2 + half) * CELL, source.astype(jnp.float32))

    def step(at, carry):
        stage, pair = at // 2, lax.rem(at, 2)
        block = stage // 2
        lat_window = jnp.where(block == 0, stage, 3 - stage)

        @pl.when(lax.rem(at, 4) == 0)
        def _():
            wait_sibling(block)
            spread_tables(block, gathered, spread, tables)

        @pl.when(at == 4)
        def _():
            widen(2, 0, sent[3, 1])
            for i in (3, 1, 0):
                ahead[i].wait_recv()
            widen(2, 1, received[2])
            widen(3, 0, received[3])
            widen(3, 1, received[4])

        @pl.when(at == 6)
        def _():
            widen(0, 0, sent[1, 1])
            widen(1, 0, sent[2, 1])
            ahead[2].wait_recv()
            ahead[4].wait_recv()
            widen(0, 1, received[0])
            widen(1, 1, received[1])

        run_windows(block, lat_window, pair, x, y, tables, consts, weights, lat)

        @pl.when(at == 1)
        def _():
            narrow(sent, (0, 1))
            for i in (0, 1, 2):
                ahead[i].start()
            wait_peers(1)
            sibling_copy(1).start()

        @pl.when(at == 3)
        def _():
            narrow(sent, (2, 3))
            for i in (3, 4):
                ahead[i].start()

        @pl.when(at == 5)
        def _():
            narrow(back, (2, 3))
            for i in (0, 1, 2):
                home[i].start()

        @pl.when(at == 7)
        def _():
            narrow(back, (0, 1))
            home[3].start()

        return carry

    lax.fori_loop(0, 8, step, 0)

    def put(strip, half, cells):
        for inner in range(3):
            for col in range(6):
                at = (inner * 6 + col) * 8
                lane = (half * 6 + col) * C
                out[strip * 3 + inner, :, lane : lane + C] = cells[at : at + 8].astype(jnp.bfloat16)

    for strip in range(3):
        put(strip + 1, 1, back[strip, 0].astype(jnp.float32))
    for copy in ahead:
        copy.wait_send()
    for block in range(2):
        for i in range(4):
            own_copy(block, i).wait_send()
        for i in range(3):
            passed_copy(block, i).wait_send()
        sibling_copy(block).wait_send()
    for copy in home[:3]:
        copy.wait()
    put(3, 0, returned[2].astype(jnp.float32))
    put(0, 1, returned[3].astype(jnp.float32))
    put(0, 0, returned[4].astype(jnp.float32))
    home[3].wait()
    for strip in range(2):
        put(strip + 1, 0, returned[strip].astype(jnp.float32))


def body(
    tokens,
    surface_ids,
    surface_embed,
    type_index,
    bias_plain,
    bias_shift,
    w_qkv,
    w_proj,
    w_up,
    w_down,
):
    spread = jnp.asarray(spread_matrix(), jnp.bfloat16)
    tail = jnp.asarray(query_tail(), jnp.float32)
    masks = jnp.asarray(mask_rows(), jnp.float32)
    lanes = jnp.asarray(head_lanes(), jnp.float32)
    in_vmem = pl.BlockSpec(memory_space=pltpu.VMEM)
    in_smem = pl.BlockSpec(memory_space=pltpu.SMEM)
    anywhere = pl.BlockSpec(memory_space=pl.ANY)
    rows = pl.pallas_call(
        kernel,
        out_shape=jax.ShapeDtypeStruct((ROWS, Z, COLS * C), jnp.bfloat16),
        in_specs=[anywhere, in_smem, in_smem]
        + [in_vmem] * 3
        + [anywhere]
        + [in_vmem] * 3
        + [anywhere] * 4,
        out_specs=in_vmem,
        scratch_shapes=[
            pltpu.VMEM((ROWS, Z, COLS * C), jnp.bfloat16),
            pltpu.VMEM((8, C), jnp.float32),
            pltpu.VMEM((2, 1104, 128), jnp.float32),
            pltpu.VMEM((4, 128, 384), jnp.bfloat16),
            pltpu.VMEM((3, 64, 128), jnp.float32),
            pltpu.VMEM((2, 48, 384), jnp.bfloat16),
            pltpu.VMEM((2, 6, 256, 256), jnp.bfloat16),
            pltpu.VMEM((2, C, 3 * C), jnp.bfloat16),
            pltpu.VMEM((2, C, HEADS * 128), jnp.bfloat16),
            pltpu.VMEM((2, C, C), jnp.bfloat16),
            pltpu.VMEM((2, C, C), jnp.bfloat16),
            pltpu.VMEM((2, C, 4 * C), jnp.bfloat16),
            pltpu.VMEM((2, 4 * C, C), jnp.bfloat16),
            pltpu.VMEM((2, 2, 4, 2, 48, 384), jnp.bfloat16),
            pltpu.VMEM((TABLES, WW, 16, 256), jnp.bfloat16),
            pltpu.VMEM((2, TOKENS, 128), jnp.float32),
            pltpu.VMEM((2, TOKENS, 128), jnp.float32),
            pltpu.VMEM((STRIPS, 2, CELL, C), jnp.bfloat16),
            pltpu.VMEM((5, CELL, C), jnp.bfloat16),
            pltpu.VMEM((STRIPS, 2, CELL, C), jnp.bfloat16),
            pltpu.VMEM((5, CELL, C), jnp.bfloat16),
            pltpu.SemaphoreType.DMA((6,)),
            pltpu.SemaphoreType.DMA((2, 8)),
            pltpu.SemaphoreType.DMA((2, 8)),
            pltpu.SemaphoreType.DMA((9,)),
            pltpu.SemaphoreType.DMA((9,)),
        ],
        compiler_params=pltpu.CompilerParams(
            collective_id=0, has_side_effects=True, vmem_limit_bytes=56 * 1024 * 1024
        ),
    )(
        tokens.transpose(1, 0, 2),
        surface_ids,
        type_index,
        surface_embed,
        bias_plain.reshape(SHARD_LINES, 128),
        bias_shift.reshape(SHARD_LINES, 128),
        spread,
        tail,
        masks,
        lanes,
        w_qkv.reshape(2, C, 3 * C),
        w_proj.reshape(2, C, C),
        w_up,
        w_down.reshape(2, 4 * C, C),
    )
    return rows.transpose(1, 0, 2)


def solution(mesh):
    return jax.shard_map(
        body,
        mesh=mesh,
        in_specs=(
            P(None, "lat", "lon"),
            P("lat", "lon"),
            P(),
            P("lat"),
            P("lon"),
            P("lon"),
            P(),
            P(),
            P(),
            P(),
        ),
        out_specs=P(None, "lat", "lon"),
        check_vma=False,
    )
```

time: 77.6 us -> 62 us (0.80)
  Pallas kernels: 61.5 us -> 54.1 us
  local copies, waits for them, and re-layouts: 12.3 us -> 7.71 us
  other arithmetic: 2.59 us -> 0 us
  matrix products: 0.86 us -> 0 us
    pallas_call x1, Pallas kernels: 61.5 us -> 54.1 us  [body(): pl.pallas_call(kernel, out_shape=jax.ShapeDtypeStruct((ROWS, Z, COLS * C)...]
    another operation x2 -> x0, local copies, waits for them, and re-layouts: 2.37 us -> none  [pick_types(): jnp.stack([bias_plain.reshape(SHARD_ROWS, -1), bias_shift.reshape(SHARD_R...]
    slice x3 -> x0, local copies, waits for them, and re-layouts: 2.21 us -> none  [the longest x1 1.32 us: pick_types(): wanted = jnp.where(lane < KAPPA, type_index[0], type_index[1])]
    convert_element_type x1 -> x0, other arithmetic: 1.27 us -> none  [body(): surface_embed.astype(jnp.float32)]
    add x1 -> x0, other arithmetic: 1.27 us -> none  [pick_types(): choose = (entry == relative * TYPES + wanted) & (lane < 2 * KAPPA)]
    reshape x1, local copies, waits for them, and re-layouts: 0.9 us -> 1.86 us  [body(): w_proj.reshape(2, C, C)]
    dot_general x1 -> x0, matrix products: 0.86 us -> none  [pick_types(): jnp.dot(both.reshape(2 * SHARD_ROWS, -1), choose.astype(jnp.bfloat16), pr...]
    transpose x1 -> x0, local copies, waits for them, and re-layouts: 0.82 us -> none  [body(): w_kt = qkv[:, :, C:2 * C].transpose(0, 2, 1)]
where the time goes in v2:
time: 62 us; the launch traced here: 61.8 us
  Pallas kernels  54.1 us (87%)
  local copies, waits for them, and re-layouts  7.71 us (12%)
    pallas_call x1, Pallas kernels, body(): pl.pallas_call(kernel, out_shape=jax.ShapeDtypeStruct((ROWS, Z, COLS * C)...  54.1 us
    reshape x1, local copies, waits for them, and re-layouts, body(): w_qkv.reshape(2, C, 3 * C)  2.27 us
    reshape x1, local copies, waits for them, and re-layouts, body(): w_proj.reshape(2, C, C)  1.86 us
    unnamed x3, local copies, waits for them, and re-layouts  1.81 us
    reshape x1, local copies, waits for them, and re-layouts, body(): w_down.reshape(2, 4 * C, C)  1.77 us

profile of v2, /device:TPU:0, one launch (start us, length us, event | category | flops | bytes accessed | tf_op | source)
XLA Modules:
  0.0 61.8 jit_solution(13002224614400052074)
XLA Ops:
  0.0 0.0 copy-start
  0.0 1.9 %reshape.18.proj_hbm = bf16[2,192,192]{2,1,0:T(8,128)(2,1)} reshape(bf16[2,36864]{1,0:T(2,128)(2,1)} %param.21) | data formatting | bytes 294912 | tf_op jit(solution)/shard_map/reshape | solution.py:619
  1.9 2.3 %reshape.17.qkv_hbm = bf16[2,192,576]{2,1,0:T(8,128)(2,1)} reshape(bf16[2,110592]{1,0:T(2,128)(2,1)} %param.20) | data formatting | bytes 884736 | tf_op jit(solution)/shard_map/reshape | solution.py:618
  4.1 0.0 copy-done
  4.1 1.8 %reshape.19.down_hbm = bf16[2,768,192]{2,1,0:T(8,128)(2,1)} reshape(bf16[2,147456]{1,0:T(2,128)(2,1)S(1)} %copy-done) | data formatting | bytes 1179648 | tf_op jit(solution)/shard_map/reshape | solution.py:621
  5.9 54.1 %shard_map.136 = bf16[12,8,2304]{2,1,0:T(8,128)(2,1)} custom-call(bf16[12,8,2304]{2,1,0:T(8,128)(2,1)} %bitcast.5, s32[12,12]{1,0:T(8,128)} %ids.1, s32[2]{0:T(128)} %types.1, bf16[3,192]{1,0:T(4,128)(2,1)} %embed_in.1, bf16[621,128]{1,0:T(8,128)(2,1)} %bitcast.6, bf16[621,128]{1,0:T(8,128)(2,1)} %bitcast.7, ...), custom_call_target="tpu_custom_call" | custom-call | tf_op jit(solution)/shard_map/pallas_call | solution.py:567
  60.0 1.8 %copy.16 = bf16[8,12,2304]{2,0,1:T(8,128)(2,1)} copy(bf16[8,12,2304]{2,0,1:T(8,128)(2,1)} %bitcast.4) | data formatting | bytes 884736
Async XLA Ops:
  0.0 4.1 %copy-start = (bf16[2,147456]{1,0:T(2,128)(2,1)S(1)}, bf16[2,147456]{1,0:T(2,128)(2,1)}, u32[]{:S(2)}) copy-start(bf16[2,147456]{1,0:T(2,128)(2,1)} %param.23) | copy-start | bytes 1769476

commit v3 on v2

--- a/solution.py
+++ b/solution.py
@@ -73,9 +73,19 @@
 
 
 def head_lanes():
-    out = np.zeros((HEADS, 1, C), np.float32)
+    out = np.zeros((HEADS + 1, 1, 256), np.float32)
     for head in range(HEADS):
         out[head, 0, head * HEAD_DIM : (head + 1) * HEAD_DIM] = 1.0
+        out[head, 0, C + head] = 1.0
+        out[HEADS, 0, C + head] = 1.0
+    return out
+
+
+def head_spread():
+    out = np.zeros((256, C), np.float32)
+    for head in range(HEADS):
+        for row in (64 + head, 192 + head):
+            out[row, head * HEAD_DIM : (head + 1) * HEAD_DIM] = 1.0
     return out
 
 
@@ -91,8 +101,11 @@
 
 
 def gelu(v):
-    inner = v * (0.7978845608028654 + (0.7978845608028654 * 0.044715) * (v * v))
-    return v * (0.5 + 0.5 * jnp.tanh(inner))
+    v = v.astype(jnp.bfloat16)
+    first, third = jnp.bfloat16(0.7978845608028654), jnp.bfloat16(0.7978845608028654 * 0.044715)
+    grown = jnp.tanh(v * (first + third * (v * v)))
+    half = jnp.bfloat16(0.5) * v
+    return half + half * grown
 
 
 def dot(a, b):
@@ -166,7 +179,7 @@
         choose[phase] = (row == target).astype(jnp.float32).astype(jnp.bfloat16)
 
 
-def prepare_weights(qkv, w_q, w_kt):
+def prepare_weights(qkv, w_q, w_kt, w_v):
     lane = lax.broadcasted_iota(jnp.int32, (1, HEADS * 128), 1)
     inner = lax.rem(lane, 128)
     target = jnp.where(inner < HEAD_DIM, (lane // 128) * HEAD_DIM + inner, -1)
@@ -177,6 +190,8 @@
     for block in range(2):
         w_q[block] = dot(qkv[block, :, 0:C], place).astype(jnp.bfloat16)
         w_kt[block] = dot_nt(one, qkv[block, :, C : 2 * C]).astype(jnp.bfloat16)
+        blank = jnp.zeros((C, 256 - C), jnp.bfloat16)
+        w_v[block] = jnp.concatenate([qkv[block, :, 2 * C : 3 * C], blank], axis=1)
 
 
 def spread_tables(block, gathered, spread, tables):
@@ -211,7 +226,7 @@
 
 
 def run_windows(block, lat_window, pair, x, y, tables, consts, weights, band):
-    tail, masks, lanes = consts
+    tail, masks, lanes, across_heads = consts
     w_q, w_kt, w_v, w_proj, w_up, w_down = weights
     last_band = (band == lax.axis_size("lat") - 1).astype(jnp.float32)
     shifted = block.astype(jnp.float32)
@@ -234,7 +249,7 @@
         second = normed[(2 * i + 1) * HALF : (2 * i + 2) * HALF]
         padded = jnp.concatenate([first, blank, second, blank], axis=0).astype(jnp.bfloat16)
         keys = dot_nt(w_kt[block], padded).astype(jnp.bfloat16)
-        values = dot(padded, w_v[block, :, 2 * C : 3 * C]).astype(jnp.bfloat16)
+        values = (dot(padded, w_v[block]) + lanes[HEADS]).astype(jnp.bfloat16)
         on_level = (level_windows[i] == 3).astype(jnp.float32) * shifted
         on_lat = (lat_window == 1).astype(jnp.float32) * last_band * shifted
         mask = masks[0] + masks[1] * on_level + masks[2] * on_lat
@@ -249,17 +264,23 @@
             right = jnp.concatenate([keys[32 * head : 32 * head + 32], table, mask], axis=0)
             scores = dot(left, right)
             top = jnp.max(scores, axis=-1, keepdims=True)
-            grown = jnp.exp(scores - top)
-            total = jnp.sum(grown, axis=-1, keepdims=True)
-            weight_parts.append((grown * (1.0 / total)).astype(jnp.bfloat16))
+            weight_parts.append(jnp.exp((scores - top).astype(jnp.bfloat16)))
             value_parts.append(values * lanes[head].astype(jnp.bfloat16))
         mixed_all.append(
             dot(jnp.concatenate(weight_parts, axis=1), jnp.concatenate(value_parts, axis=0))
         )
-    mixed = jnp.concatenate(mixed_all, axis=0).astype(jnp.bfloat16)
+    mixed = jnp.concatenate(mixed_all, axis=0)
+    totals = mixed[:, 128:256]
+    lane = lax.broadcasted_iota(jnp.int32, totals.shape, 1)
+    counted = (lane >= C - 128) & (lane < C - 128 + HEADS)
+    inverse = jnp.where(counted, 1.0 / totals, 0.0)
+    coarse = inverse.astype(jnp.bfloat16)
+    fine = (inverse - coarse.astype(jnp.float32)).astype(jnp.bfloat16)
+    scale = dot(jnp.concatenate([coarse, fine], axis=1), across_heads[...])
+    mixed = (mixed[:, :C] * scale).astype(jnp.bfloat16)
     middle = rounded(stream + dot(mixed, w_proj[block]))
     lifted = gelu(dot(normalised(middle).astype(jnp.bfloat16), w_up[block]))
-    result = middle + dot(lifted.astype(jnp.bfloat16), w_down[block])
+    result = middle + dot(lifted, w_down[block])
     for j, s in enumerate(starts):
         put_strided(y, s, result[j * HALF : (j + 1) * HALF])
 
@@ -275,6 +296,7 @@
     tail,
     masks,
     lanes,
+    across_heads,
     qkv_hbm,
     proj_hbm,
     up_hbm,
@@ -290,6 +312,7 @@
     qkv,
     w_q,
     w_kt,
+    w_v,
     w_proj,
     w_up,
     w_down,
@@ -309,8 +332,8 @@
 ):
     lat, lon = lax.axis_index("lat"), lax.axis_index("lon")
     lats, lons = lax.axis_size("lat"), lax.axis_size("lon")
-    consts = (tail, masks, lanes)
-    weights = (w_q, w_kt, qkv, w_proj, w_up, w_down)
+    consts = (tail, masks, lanes, across_heads)
+    weights = (w_q, w_kt, w_v, w_proj, w_up, w_down)
     north, south = lax.rem(lat + lats - 1, lats), lax.rem(lat + 1, lats)
     west, east = lax.rem(lon + lons - 1, lons), lax.rem(lon + 1, lons)
 
@@ -389,14 +412,13 @@
     choose_lanes(types, choose)
     pl.semaphore_wait(barrier, len(partners))
 
-    def pick_and_send(block, carry):
+    def pick_and_send(block):
         pick_types(block, lines, types, choose, ordered, picked)
         for i in range(4):
             own_copy(block, i).start()
         gathered[block, core, x_at, z_at] = picked[block]
-        return carry
-
-    lax.fori_loop(0, 2, pick_and_send, 0)
+
+    pick_and_send(0)
 
     embed[0:3, :] = embed_in[...].astype(jnp.float32)
     loads[0].wait()
@@ -419,10 +441,10 @@
 
     pass_on(0)
     loads[1].wait()
-    prepare_weights(qkv, w_q, w_kt)
-    pass_on(1)
+    prepare_weights(qkv, w_q, w_kt, w_v)
     wait_peers(0)
     sibling_copy(0).start()
+    pick_and_send(1)
     for load in loads[2:]:
         load.wait()
 
@@ -488,6 +510,10 @@
             widen(1, 1, received[1])
 
         run_windows(block, lat_window, pair, x, y, tables, consts, weights, lat)
+
+        @pl.when(at == 0)
+        def _():
+            pass_on(1)
 
         @pl.when(at == 1)
         def _():
@@ -570,7 +596,7 @@
         in_specs=[anywhere, in_smem, in_smem]
         + [in_vmem] * 3
         + [anywhere]
-        + [in_vmem] * 3
+        + [in_vmem] * 4
         + [anywhere] * 4,
         out_specs=in_vmem,
         scratch_shapes=[
@@ -584,6 +610,7 @@
             pltpu.VMEM((2, C, 3 * C), jnp.bfloat16),
             pltpu.VMEM((2, C, HEADS * 128), jnp.bfloat16),
             pltpu.VMEM((2, C, C), jnp.bfloat16),
+            pltpu.VMEM((2, C, 256), jnp.bfloat16),
             pltpu.VMEM((2, C, C), jnp.bfloat16),
             pltpu.VMEM((2, C, 4 * C), jnp.bfloat16),
             pltpu.VMEM((2, 4 * C, C), jnp.bfloat16),
@@ -615,6 +642,7 @@
         tail,
         masks,
         lanes,
+        jnp.asarray(head_spread(), jnp.bfloat16),
         w_qkv.reshape(2, C, 3 * C),
         w_proj.reshape(2, C, C),
         w_up,

time: 62 us -> 60.6 us (0.977)
  Pallas kernels: 54.1 us -> 52.6 us
    pallas_call x1, Pallas kernels: 54.1 us -> 52.6 us  [body(): pl.pallas_call(kernel, out_shape=jax.ShapeDtypeStruct((ROWS, Z, COLS * C)...]
where the time goes in v3:
time: 60.6 us; the launch traced here: 60.3 us
  Pallas kernels  52.6 us (87%)
  local copies, waits for them, and re-layouts  7.71 us (13%)
    pallas_call x1, Pallas kernels, body(): pl.pallas_call(kernel, out_shape=jax.ShapeDtypeStruct((ROWS, Z, COLS * C)...  52.6 us
    reshape x1, local copies, waits for them, and re-layouts, body(): w_qkv.reshape(2, C, 3 * C)  2.27 us
    reshape x1, local copies, waits for them, and re-layouts, body(): w_proj.reshape(2, C, C)  1.86 us
    unnamed x3, local copies, waits for them, and re-layouts  1.81 us
    reshape x1, local copies, waits for them, and re-layouts, body(): w_down.reshape(2, 4 * C, C)  1.77 us

profile of v3, /device:TPU:0, one launch (start us, length us, event | category | flops | bytes accessed | tf_op | source)
XLA Modules:
  0.0 60.3 jit_solution(14738328699629745412)
XLA Ops:
  0.0 0.0 copy-start
  0.0 1.9 %reshape.18.proj_hbm = bf16[2,192,192]{2,1,0:T(8,128)(2,1)} reshape(bf16[2,36864]{1,0:T(2,128)(2,1)} %param.22) | data formatting | bytes 294912 | tf_op jit(solution)/shard_map/reshape | solution.py:647
  1.9 2.3 %reshape.17.qkv_hbm = bf16[2,192,576]{2,1,0:T(8,128)(2,1)} reshape(bf16[2,110592]{1,0:T(2,128)(2,1)} %param.21) | data formatting | bytes 884736 | tf_op jit(solution)/shard_map/reshape | solution.py:646
  4.1 0.0 copy-done
  4.1 1.8 %reshape.19.down_hbm = bf16[2,768,192]{2,1,0:T(8,128)(2,1)} reshape(bf16[2,147456]{1,0:T(2,128)(2,1)S(1)} %copy-done) | data formatting | bytes 1179648 | tf_op jit(solution)/shard_map/reshape | solution.py:649
  5.9 52.6 %shard_map.145 = bf16[12,8,2304]{2,1,0:T(8,128)(2,1)} custom-call(bf16[12,8,2304]{2,1,0:T(8,128)(2,1)} %bitcast.5, s32[12,12]{1,0:T(8,128)} %ids.1, s32[2]{0:T(128)} %types.1, bf16[3,192]{1,0:T(4,128)(2,1)} %embed_in.1, bf16[621,128]{1,0:T(8,128)(2,1)} %bitcast.6, bf16[621,128]{1,0:T(8,128)(2,1)} %bitcast.7, ...), custom_call_target="tpu_custom_call" | custom-call | tf_op jit(solution)/shard_map/pallas_call | solution.py:593
  58.5 1.8 %copy.17 = bf16[8,12,2304]{2,0,1:T(8,128)(2,1)} copy(bf16[8,12,2304]{2,0,1:T(8,128)(2,1)} %bitcast.4) | data formatting | bytes 884736
Async XLA Ops:
  0.0 4.1 %copy-start = (bf16[2,147456]{1,0:T(2,128)(2,1)S(1)}, bf16[2,147456]{1,0:T(2,128)(2,1)}, u32[]{:S(2)}) copy-start(bf16[2,147456]{1,0:T(2,128)(2,1)} %param.24) | copy-start | bytes 1769476

commit v4 on v3

--- a/solution.py
+++ b/solution.py
@@ -179,7 +179,40 @@
         choose[phase] = (row == target).astype(jnp.float32).astype(jnp.bfloat16)
 
 
-def prepare_weights(qkv, w_q, w_kt, w_v):
+def to_lines(flat, lines):
+    count = flat.shape[1] // 128
+
+    def step(at, carry):
+        start = pl.multiple_of(at * 2048, 2048)
+        chunk = flat[:, pl.ds(start, 2048)].astype(jnp.float32)
+        for j in range(16):
+            for block in range(2):
+                lines[block, pl.ds(at * 16 + j, 1), :] = chunk[
+                    block : block + 1, 128 * j : 128 * j + 128
+                ]
+        return carry
+
+    lax.fori_loop(0, count // 16, step, 0)
+
+
+def to_matrix(lines, wide, block, rows, columns):
+    period = 2 * columns // 128
+    parts = [lines[block, pl.ds(j, rows // 2, stride=period), :] for j in range(period)]
+    middle = period // 2
+    full = columns // 128
+    for tile in range(full):
+        wide[tile, pl.ds(0, rows // 2, stride=2), :] = parts[tile]
+        wide[tile, pl.ds(1, rows // 2, stride=2), :] = jnp.concatenate(
+            [parts[middle + tile][:, 64:], parts[middle + tile + 1][:, :64]], axis=1
+        )
+    wide[full, pl.ds(0, rows // 2, stride=2), :] = parts[middle]
+    last = parts[period - 1]
+    wide[full, pl.ds(1, rows // 2, stride=2), :] = jnp.concatenate([last[:, 64:], last[:, :64]], axis=1)
+    pieces = [wide[tile, 0:rows, :] for tile in range(full)] + [wide[full, 0:rows, 0:64]]
+    return jnp.concatenate(pieces, axis=1).astype(jnp.bfloat16)
+
+
+def prepare_weights(lines, wide, w_q, w_kt, w_v):
     lane = lax.broadcasted_iota(jnp.int32, (1, HEADS * 128), 1)
     inner = lax.rem(lane, 128)
     target = jnp.where(inner < HEAD_DIM, (lane // 128) * HEAD_DIM + inner, -1)
@@ -188,10 +221,11 @@
     one = lax.broadcasted_iota(jnp.int32, (C, C), 0) == lax.broadcasted_iota(jnp.int32, (C, C), 1)
     one = one.astype(jnp.float32).astype(jnp.bfloat16)
     for block in range(2):
-        w_q[block] = dot(qkv[block, :, 0:C], place).astype(jnp.bfloat16)
-        w_kt[block] = dot_nt(one, qkv[block, :, C : 2 * C]).astype(jnp.bfloat16)
+        qkv = to_matrix(lines, wide, block, C, 3 * C)
+        w_q[block] = dot(qkv[:, 0:C], place).astype(jnp.bfloat16)
+        w_kt[block] = dot_nt(one, qkv[:, C : 2 * C]).astype(jnp.bfloat16)
         blank = jnp.zeros((C, 256 - C), jnp.bfloat16)
-        w_v[block] = jnp.concatenate([qkv[block, :, 2 * C : 3 * C], blank], axis=1)
+        w_v[block] = jnp.concatenate([qkv[:, 2 * C : 3 * C], blank], axis=1)
 
 
 def spread_tables(block, gathered, spread, tables):
@@ -316,6 +350,12 @@
     w_proj,
     w_up,
     w_down,
+    flat_proj,
+    flat_down,
+    qkv_lines,
+    proj_lines,
+    down_lines,
+    wide,
     gathered,
     tables,
     x,
@@ -338,7 +378,7 @@
     west, east = lax.rem(lon + lons - 1, lons), lax.rem(lon + 1, lons)
 
     sources = (tokens_hbm, qkv_hbm, spread_hbm, proj_hbm, up_hbm, down_hbm)
-    targets = (tokens, qkv, spread, w_proj, w_up, w_down)
+    targets = (tokens, qkv, spread, flat_proj, w_up, flat_down)
     loads = [
         pltpu.make_async_copy(source, target, local_sems.at[i])
         for i, (source, target) in enumerate(zip(sources, targets))
@@ -441,12 +481,21 @@
 
     pass_on(0)
     loads[1].wait()
-    prepare_weights(qkv, w_q, w_kt, w_v)
+    to_lines(qkv, qkv_lines)
+    prepare_weights(qkv_lines, wide, w_q, w_kt, w_v)
+    loads[3].wait()
+    to_lines(flat_proj, proj_lines)
+    for block in range(2):
+        w_proj[block] = to_matrix(proj_lines, wide, block, C, C)
     wait_peers(0)
     sibling_copy(0).start()
     pick_and_send(1)
-    for load in loads[2:]:
-        load.wait()
+    loads[5].wait()
+    to_lines(flat_down, down_lines)
+    for block in range(2):
+        w_down[block] = to_matrix(down_lines, wide, block, 4 * C, C)
+    loads[2].wait()
+    loads[4].wait()
 
     def halo(index, source, target, i, j):
         return pltpu.make_async_remote_copy(
@@ -607,13 +656,19 @@
             pltpu.VMEM((3, 64, 128), jnp.float32),
             pltpu.VMEM((2, 48, 384), jnp.bfloat16),
             pltpu.VMEM((2, 6, 256, 256), jnp.bfloat16),
-            pltpu.VMEM((2, C, 3 * C), jnp.bfloat16),
+            pltpu.VMEM((2, 3 * C * C), jnp.bfloat16),
             pltpu.VMEM((2, C, HEADS * 128), jnp.bfloat16),
             pltpu.VMEM((2, C, C), jnp.bfloat16),
             pltpu.VMEM((2, C, 256), jnp.bfloat16),
             pltpu.VMEM((2, C, C), jnp.bfloat16),
             pltpu.VMEM((2, C, 4 * C), jnp.bfloat16),
             pltpu.VMEM((2, 4 * C, C), jnp.bfloat16),
+            pltpu.VMEM((2, C * C), jnp.bfloat16),
+            pltpu.VMEM((2, 4 * C * C), jnp.bfloat16),
+            pltpu.VMEM((2, 3 * C * C // 128, 128), jnp.float32),
+            pltpu.VMEM((2, C * C // 128, 128), jnp.float32),
+            pltpu.VMEM((2, 4 * C * C // 128, 128), jnp.float32),
+            pltpu.VMEM((5, 4 * C, 128), jnp.float32),
             pltpu.VMEM((2, 2, 4, 2, 48, 384), jnp.bfloat16),
             pltpu.VMEM((TABLES, WW, 16, 256), jnp.bfloat16),
             pltpu.VMEM((2, TOKENS, 128), jnp.float32),
@@ -643,10 +698,10 @@
         masks,
         lanes,
         jnp.asarray(head_spread(), jnp.bfloat16),
-        w_qkv.reshape(2, C, 3 * C),
-        w_proj.reshape(2, C, C),
+        w_qkv,
+        w_proj,
         w_up,
-        w_down.reshape(2, 4 * C, C),
+        w_down,
     )
     return rows.transpose(1, 0, 2)
 

time: 60.6 us -> 55.4 us (0.914)
  local copies, waits for them, and re-layouts: 7.71 us -> 1.8 us
  Pallas kernels: 52.6 us -> 53.5 us
    reshape x3 -> x0, local copies, waits for them, and re-layouts: 5.91 us -> none  [the longest x1 2.27 us: body(): w_qkv.reshape(2, C, 3 * C)]
    pallas_call x1, Pallas kernels: 52.6 us -> 53.5 us  [body(): pl.pallas_call(kernel, out_shape=jax.ShapeDtypeStruct((ROWS, Z, COLS * C)...]
    unnamed x3 -> x1, local copies, waits for them, and re-layouts: 1.81 us -> 1.8 us
where the time goes in v4:
time: 55.4 us; the launch traced here: 55.3 us
  Pallas kernels  53.5 us (97%)
  local copies, waits for them, and re-layouts  1.8 us (3%)
    pallas_call x1, Pallas kernels, body(): pl.pallas_call(kernel, out_shape=jax.ShapeDtypeStruct((ROWS, Z, COLS * C)...  53.5 us
    unnamed x1, local copies, waits for them, and re-layouts  1.8 us

profile of v4, /device:TPU:0, one launch (start us, length us, event | category | flops | bytes accessed | tf_op | source)
XLA Modules:
  0.0 55.3 jit_solution(1382832668707534089)
XLA Ops:
  0.0 53.5 %shard_map.145 = bf16[12,8,2304]{2,1,0:T(8,128)(2,1)} custom-call(bf16[12,8,2304]{2,1,0:T(8,128)(2,1)} %bitcast.5, s32[12,12]{1,0:T(8,128)} %ids.1, s32[2]{0:T(128)} %types.1, bf16[3,192]{1,0:T(4,128)(2,1)} %embed_in.1, bf16[621,128]{1,0:T(8,128)(2,1)} %bitcast.6, bf16[621,128]{1,0:T(8,128)(2,1)} %bitcast.7, ...), custom_call_target="tpu_custom_call" | custom-call | tf_op jit(solution)/shard_map/pallas_call | solution.py:642
  53.5 1.8 %copy.17 = bf16[8,12,2304]{2,0,1:T(8,128)(2,1)} copy(bf16[8,12,2304]{2,0,1:T(8,128)(2,1)} %bitcast.4) | data formatting | bytes 884736

commit v5 on v4

--- a/solution.py
+++ b/solution.py
@@ -116,16 +116,20 @@
     return lax.dot_general(a, b, (((1,), (1,)), ((), ())), preferred_element_type=jnp.float32)
 
 
+def row_of(level, lat_window):
+    return (level // 4) * (TOKENS // 2) + lat_window * (HALF * 4) + lax.rem(level, 4)
+
+
 def take_strided(ref, start):
-    near = ref[0, pl.ds(start, HALF, stride=8), :]
-    far = ref[1, pl.ds(start, HALF, stride=8), :]
+    near = ref[0, pl.ds(start, HALF, stride=4), :]
+    far = ref[1, pl.ds(start, HALF, stride=4), :]
     return jnp.concatenate([near, far[:, : C - 128]], axis=1)
 
 
 def put_strided(ref, start, value):
     blank = jnp.zeros((HALF, 256 - C), jnp.float32)
-    ref[0, pl.ds(start, HALF, stride=8), :] = value[:, :128]
-    ref[1, pl.ds(start, HALF, stride=8), :] = jnp.concatenate([value[:, 128:], blank], axis=1)
+    ref[0, pl.ds(start, HALF, stride=4), :] = value[:, :128]
+    ref[1, pl.ds(start, HALF, stride=4), :] = jnp.concatenate([value[:, 128:], blank], axis=1)
 
 
 def take_rows(ref, start, count):
@@ -256,7 +260,7 @@
                     ] = part
             return carry
 
-        lax.fori_loop(0, 6, step, 0)
+        lax.fori_loop(0, 6, step, 0, unroll=3)
 
 
 def run_windows(block, lat_window, pair, x, y, tables, consts, weights, band):
@@ -264,13 +268,15 @@
     w_q, w_kt, w_v, w_proj, w_up, w_down = weights
     last_band = (band == lax.axis_size("lat") - 1).astype(jnp.float32)
     shifted = block.astype(jnp.float32)
-    starts, level_windows = [], []
+    starts, ends, level_windows = [], [], []
     for i in range(PAIR):
         level_window = pair * PAIR + i
         level_windows.append(level_window)
         for a in range(2):
-            level = lax.rem(2 * level_window + a + block, Z)
-            starts.append(lat_window * (HALF * Z) + level)
+            rolled = 2 * level_window + a
+            level = lax.rem(rolled + block, Z)
+            starts.append(row_of(level, lat_window))
+            ends.append(row_of(rolled, lat_window))
     parts = [take_strided(x, s) for s in starts]
     stream = jnp.concatenate(parts, axis=0)
     normed = normalised(stream)
@@ -315,7 +321,7 @@
     middle = rounded(stream + dot(mixed, w_proj[block]))
     lifted = gelu(dot(normalised(middle).astype(jnp.bfloat16), w_up[block]))
     result = middle + dot(lifted, w_down[block])
-    for j, s in enumerate(starts):
+    for j, s in enumerate(ends):
         put_strided(y, s, result[j * HALF : (j + 1) * HALF])
 
 
@@ -360,9 +366,8 @@
     tables,
     x,
     y,
-    sent,
+    moved,
     received,
-    back,
     returned,
     local_sems,
     gather_send,
@@ -465,11 +470,16 @@
 
     def embed_row(row, carry):
         strip, inner = row // 3, row % 3
-        for col in range(COLS):
-            cell = tokens[row, :, C * col : C * col + C].astype(jnp.float32)
-            line = embed[pl.ds(ids[row, col], 1), :]
-            start = ((strip * 2 + col // 6) * 18 + inner * 6 + col % 6) * 8
-            put_rows(x, pl.multiple_of(start, 8), rounded(cell + line))
+        for col in range(0, COLS, 2):
+            cells = []
+            for c in (col, col + 1):
+                cell = tokens[row, :, C * c : C * c + C].astype(jnp.float32)
+                cells.append(rounded(cell + embed[pl.ds(ids[row, c], 1), :]))
+            for part in range(2):
+                start = part * (TOKENS // 2) + (strip * 2 + col // 6) * HALF
+                start = pl.multiple_of(start + (inner * 6 + col % 6) * 4, 8)
+                rows = [cell[4 * part : 4 * part + 4] for cell in cells]
+                put_rows(x, start, jnp.concatenate(rows, axis=0))
         return carry
 
     lax.fori_loop(0, ROWS, embed_row, 0)
@@ -507,28 +517,37 @@
             device_id_type=pl.DeviceIdType.MESH,
         )
 
+    sent, back = moved.at[0], moved.at[1]
     ahead = [
-        halo(0, sent.at[0, 0], received.at[4], north, west),
-        halo(1, sent.at[0, 1], received.at[3], north, lon),
-        halo(2, sent.at[1, 0], received.at[0], lat, west),
-        halo(3, sent.at[3, 0], received.at[2], lat, west),
-        halo(4, sent.at[2, 0], received.at[1], lat, west),
+        halo(0, sent.at[:, 0, 0], received.at[:, 4], north, west),
+        halo(1, sent.at[:, 1, 0], received.at[:, 3], north, lon),
+        halo(2, sent.at[:, 0, 1], received.at[:, 0], lat, west),
     ]
-    home = [
-        halo(5, back.at[3, 1], returned.at[4], south, east),
-        halo(6, back.at[3, 0], returned.at[3], south, lon),
-        halo(7, back.at[2, 1], returned.at[2], lat, east),
-        halo(8, back.at[0:2, 1], returned.at[0:2], lat, east),
-    ]
-
-    def narrow(target, strips):
-        for strip in strips:
+    ahead += [halo(3 + p, sent.at[p, 0, 3], received.at[p, 2], lat, west) for p in range(2)]
+    ahead += [halo(5 + p, sent.at[p, 0, 2], received.at[p, 1], lat, west) for p in range(2)]
+    home = []
+    for p in range(2):
+        home += [
+            halo(7 + 3 * p, back.at[p, 1, 3], returned.at[p, 4], south, east),
+            halo(8 + 3 * p, back.at[p, 0, 3], returned.at[p, 3], south, lon),
+            halo(9 + 3 * p, back.at[p, 1, 2], returned.at[p, 2], lat, east),
+        ]
+    home += [halo(13 + p, back.at[p, 1, 0:2], returned.at[p, 0:2], lat, east) for p in range(2)]
+
+    def piece(p, strip, half):
+        return p * (TOKENS // 2) + (strip * 2 + half) * HALF
+
+    def narrow(block, p, lat_window):
+        blank = jnp.zeros((80 - HALF, C), jnp.float32)
+        for bh in range(2):
             for half in range(2):
-                start = (strip * 2 + half) * CELL
-                target[strip, half] = take_rows(y, start, CELL).astype(jnp.bfloat16)
-
-    def widen(strip, half, source):
-        put_rows(x, (strip * 2 + half) * CELL, source.astype(jnp.float32))
+                strip = 2 * lat_window + bh
+                rows = take_rows(y, pl.multiple_of(piece(p, strip, half), 8), HALF)
+                rows = jnp.concatenate([rows, blank], axis=0)
+                moved[block, p, half, strip] = rows.astype(jnp.bfloat16)
+
+    def widen(target, p, strip, half, source):
+        put_rows(target, piece(p, strip, half), source.astype(jnp.float32)[:HALF])
 
     def step(at, carry):
         stage, pair = at // 2, lax.rem(at, 2)
@@ -542,23 +561,43 @@
 
         @pl.when(at == 4)
         def _():
-            widen(2, 0, sent[3, 1])
-            for i in (3, 1, 0):
+            for p in range(2):
+                widen(x, p, 2, 0, sent[p, 1, 3])
+            for i in (0, 1, 3, 4):
                 ahead[i].wait_recv()
-            widen(2, 1, received[2])
-            widen(3, 0, received[3])
-            widen(3, 1, received[4])
+            for p in range(2):
+                widen(x, p, 2, 1, received[p, 2])
+                widen(x, p, 3, 0, received[p, 3])
+                widen(x, p, 3, 1, received[p, 4])
 
         @pl.when(at == 6)
         def _():
-            widen(0, 0, sent[1, 1])
-            widen(1, 0, sent[2, 1])
-            ahead[2].wait_recv()
-            ahead[4].wait_recv()
-            widen(0, 1, received[0])
-            widen(1, 1, received[1])
+            for p in range(2):
+                widen(x, p, 0, 0, sent[p, 1, 1])
+                widen(x, p, 1, 0, sent[p, 1, 2])
+            for i in (2, 5, 6):
+                ahead[i].wait_recv()
+            for p in range(2):
+                widen(x, p, 0, 1, received[p, 0])
+                widen(x, p, 1, 1, received[p, 1])
 
         run_windows(block, lat_window, pair, x, y, tables, consts, weights, lat)
+
+        narrow(block, pair, lat_window)
+
+        def after(when, copies):
+            @pl.when(at == when)
+            def _():
+                for copy in copies:
+                    copy.start()
+
+        after(1, ahead[0:3])
+        after(2, [ahead[3], ahead[5]])
+        after(3, [ahead[4], ahead[6]])
+        after(4, home[0:3])
+        after(5, home[3:6])
+        after(6, home[6:7])
+        after(7, home[7:8])
 
         @pl.when(at == 0)
         def _():
@@ -566,42 +605,39 @@
 
         @pl.when(at == 1)
         def _():
-            narrow(sent, (0, 1))
-            for i in (0, 1, 2):
-                ahead[i].start()
             wait_peers(1)
             sibling_copy(1).start()
 
-        @pl.when(at == 3)
-        def _():
-            narrow(sent, (2, 3))
-            for i in (3, 4):
-                ahead[i].start()
-
-        @pl.when(at == 5)
-        def _():
-            narrow(back, (2, 3))
-            for i in (0, 1, 2):
-                home[i].start()
-
-        @pl.when(at == 7)
-        def _():
-            narrow(back, (0, 1))
-            home[3].start()
-
         return carry
 
     lax.fori_loop(0, 8, step, 0)
 
-    def put(strip, half, cells):
-        for inner in range(3):
+    def gather_levels(p, from_strip, from_half, strip, half):
+        for near in range(4):
+            level = (4 * p + near + 1) % Z
+            for tile in range(2):
+                rows = y[tile, pl.ds(piece(p, from_strip, from_half) + near, 18, stride=4), :]
+                x[tile, pl.ds((strip * 2 + half) * CELL + level, 18, stride=8), :] = rows
+
+    def put(strip, half):
+        def put_row(inner, carry):
             for col in range(6):
-                at = (inner * 6 + col) * 8
+                at = pl.multiple_of((strip * 2 + half) * CELL + (inner * 6 + col) * 8, 8)
                 lane = (half * 6 + col) * C
-                out[strip * 3 + inner, :, lane : lane + C] = cells[at : at + 8].astype(jnp.bfloat16)
+                out[strip * 3 + inner, :, lane : lane + C] = take_rows(x, at, 8).astype(jnp.bfloat16)
+            return carry
+
+        lax.fori_loop(0, 3, put_row, 0)
+
+    def take_home(i, slot, strip, half):
+        for p in range(2):
+            widen(y, p, *slot, returned[p, i])
+            gather_levels(p, *slot, strip, half)
 
     for strip in range(3):
-        put(strip + 1, 1, back[strip, 0].astype(jnp.float32))
+        for p in range(2):
+            gather_levels(p, strip, 0, strip + 1, 1)
+        put(strip + 1, 1)
     for copy in ahead:
         copy.wait_send()
     for block in range(2):
@@ -610,14 +646,18 @@
         for i in range(3):
             passed_copy(block, i).wait_send()
         sibling_copy(block).wait_send()
-    for copy in home[:3]:
+    for copy in home[:6]:
         copy.wait()
-    put(3, 0, returned[2].astype(jnp.float32))
-    put(0, 1, returned[3].astype(jnp.float32))
-    put(0, 0, returned[4].astype(jnp.float32))
-    home[3].wait()
+    take_home(2, (2, 1), 3, 0)
+    take_home(3, (3, 0), 0, 1)
+    take_home(4, (3, 1), 0, 0)
+    for where in ((3, 0), (0, 1), (0, 0)):
+        put(*where)
+    for copy in home[6:]:
+        copy.wait()
     for strip in range(2):
-        put(strip + 1, 0, returned[strip].astype(jnp.float32))
+        take_home(strip, (strip, 1), strip + 1, 0)
+        put(strip + 1, 0)
 
 
 def body(
@@ -673,15 +713,14 @@
             pltpu.VMEM((TABLES, WW, 16, 256), jnp.bfloat16),
             pltpu.VMEM((2, TOKENS, 128), jnp.float32),
             pltpu.VMEM((2, TOKENS, 128), jnp.float32),
-            pltpu.VMEM((STRIPS, 2, CELL, C), jnp.bfloat16),
-            pltpu.VMEM((5, CELL, C), jnp.bfloat16),
-            pltpu.VMEM((STRIPS, 2, CELL, C), jnp.bfloat16),
-            pltpu.VMEM((5, CELL, C), jnp.bfloat16),
+            pltpu.VMEM((2, 2, 2, STRIPS, 80, C), jnp.bfloat16),
+            pltpu.VMEM((2, 5, 80, C), jnp.bfloat16),
+            pltpu.VMEM((2, 5, 80, C), jnp.bfloat16),
             pltpu.SemaphoreType.DMA((6,)),
             pltpu.SemaphoreType.DMA((2, 8)),
             pltpu.SemaphoreType.DMA((2, 8)),
-            pltpu.SemaphoreType.DMA((9,)),
-            pltpu.SemaphoreType.DMA((9,)),
+            pltpu.SemaphoreType.DMA((15,)),
+            pltpu.SemaphoreType.DMA((15,)),
         ],
         compiler_params=pltpu.CompilerParams(
             collective_id=0, has_side_effects=True, vmem_limit_bytes=56 * 1024 * 1024

time: 55.4 us -> 54.2 us (0.978)
  Pallas kernels: 53.5 us -> 52.2 us
    pallas_call x1, Pallas kernels: 53.5 us -> 52.2 us  [body(): pl.pallas_call(kernel, out_shape=jax.ShapeDtypeStruct((ROWS, Z, COLS * C)...]
where the time goes in v5:
time: 54.2 us; the launch traced here: 54.1 us
  Pallas kernels  52.2 us (96%)
  local copies, waits for them, and re-layouts  1.8 us (3%)
    pallas_call x1, Pallas kernels, body(): pl.pallas_call(kernel, out_shape=jax.ShapeDtypeStruct((ROWS, Z, COLS * C)...  52.2 us
    unnamed x1, local copies, waits for them, and re-layouts  1.8 us

profile of v5, /device:TPU:0, one launch (start us, length us, event | category | flops | bytes accessed | tf_op | source)
XLA Modules:
  0.0 54.1 jit_solution(17382279083124560140)
XLA Ops:
  0.0 52.2 %shard_map.145 = bf16[12,8,2304]{2,1,0:T(8,128)(2,1)} custom-call(bf16[12,8,2304]{2,1,0:T(8,128)(2,1)} %bitcast.5, s32[12,12]{1,0:T(8,128)} %ids.1, s32[2]{0:T(128)} %types.1, bf16[3,192]{1,0:T(4,128)(2,1)} %embed_in.1, bf16[621,128]{1,0:T(8,128)(2,1)} %bitcast.6, bf16[621,128]{1,0:T(8,128)(2,1)} %bitcast.7, ...), custom_call_target="tpu_custom_call" | custom-call | tf_op jit(solution)/shard_map/pallas_call | solution.py:682
  52.2 1.8 %copy.17 = bf16[8,12,2304]{2,0,1:T(8,128)(2,1)} copy(bf16[8,12,2304]{2,0,1:T(8,128)(2,1)} %bitcast.4) | data formatting | bytes 884736

commit v6 on v5

--- a/solution.py
+++ b/solution.py
@@ -260,7 +260,7 @@
                     ] = part
             return carry
 
-        lax.fori_loop(0, 6, step, 0, unroll=3)
+        lax.fori_loop(0, 6, step, 0, unroll=6)
 
 
 def run_windows(block, lat_window, pair, x, y, tables, consts, weights, band):
@@ -435,22 +435,27 @@
         held = slot(block, x_at, 1 - z_at)
         return share(block, 4 + i, held, held, peers[i])
 
-    def sibling_copy(block):
-        held = gathered.at[block, core]
-        return share(block, 7, held, held, sibling)
+    def sibling_copy(block, part):
+        held = gathered.at[block, core, :, z_at if part == 0 else 1 - z_at]
+        return share(block, 7 + part, held, held, sibling)
 
     def wait_opposite(block):
         share(block, 0, picked.at[block], slot(block, x_at, 1 - z_at), opposite).wait_recv()
 
-    def wait_peers(block):
+    def near_part(block):
         for i, origin in enumerate(origins):
             share(block, 1 + i, picked.at[block], slot(block, origin, z_at), lon).wait_recv()
+        sibling_copy(block, 0).start()
+
+    def far_part(block):
         for i, origin in enumerate(origins):
             share(block, 4 + i, picked.at[block], slot(block, origin, 1 - z_at), lon).wait_recv()
+        sibling_copy(block, 1).start()
 
     def wait_sibling(block):
-        other = gathered.at[block, 1 - core]
-        share(block, 7, other, other, sibling).wait_recv()
+        for part in range(2):
+            other = gathered.at[block, 1 - core, :, z_at if part == 0 else 1 - z_at]
+            share(block, 7 + part, other, other, sibling).wait_recv()
 
     lines[0, 0:SHARD_LINES] = bias_plain[...].astype(jnp.float32)
     lines[1, 0:SHARD_LINES] = bias_shift[...].astype(jnp.float32)
@@ -497,9 +502,9 @@
     to_lines(flat_proj, proj_lines)
     for block in range(2):
         w_proj[block] = to_matrix(proj_lines, wide, block, C, C)
-    wait_peers(0)
-    sibling_copy(0).start()
+    near_part(0)
     pick_and_send(1)
+    far_part(0)
     loads[5].wait()
     to_lines(flat_down, down_lines)
     for block in range(2):
@@ -605,8 +610,8 @@
 
         @pl.when(at == 1)
         def _():
-            wait_peers(1)
-            sibling_copy(1).start()
+            near_part(1)
+            far_part(1)
 
         return carry
 
@@ -645,7 +650,8 @@
             own_copy(block, i).wait_send()
         for i in range(3):
             passed_copy(block, i).wait_send()
-        sibling_copy(block).wait_send()
+        for part in range(2):
+            sibling_copy(block, part).wait_send()
     for copy in home[:6]:
         copy.wait()
     take_home(2, (2, 1), 3, 0)
@@ -717,8 +723,8 @@
             pltpu.VMEM((2, 5, 80, C), jnp.bfloat16),
             pltpu.VMEM((2, 5, 80, C), jnp.bfloat16),
             pltpu.SemaphoreType.DMA((6,)),
-            pltpu.SemaphoreType.DMA((2, 8)),
-            pltpu.SemaphoreType.DMA((2, 8)),
+            pltpu.SemaphoreType.DMA((2, 9)),
+            pltpu.SemaphoreType.DMA((2, 9)),
             pltpu.SemaphoreType.DMA((15,)),
             pltpu.SemaphoreType.DMA((15,)),
         ],

time: 54.2 us -> 53.7 us (level)
  no operation moved by 1% of the time
where the time goes in v6:
time: 53.7 us; the launch traced here: 53.6 us
  Pallas kernels  51.8 us (96%)
  local copies, waits for them, and re-layouts  1.8 us (3%)
    pallas_call x1, Pallas kernels, body(): pl.pallas_call(kernel, out_shape=jax.ShapeDtypeStruct((ROWS, Z, COLS * C)...  51.8 us
    unnamed x1, local copies, waits for them, and re-layouts  1.8 us

profile of v6, /device:TPU:0, one launch (start us, length us, event | category | flops | bytes accessed | tf_op | source)
XLA Modules:
  0.0 53.6 jit_solution(16480402605988902221)
XLA Ops:
  0.0 51.8 %shard_map.145 = bf16[12,8,2304]{2,1,0:T(8,128)(2,1)} custom-call(bf16[12,8,2304]{2,1,0:T(8,128)(2,1)} %bitcast.5, s32[12,12]{1,0:T(8,128)} %ids.1, s32[2]{0:T(128)} %types.1, bf16[3,192]{1,0:T(4,128)(2,1)} %embed_in.1, bf16[621,128]{1,0:T(8,128)(2,1)} %bitcast.6, bf16[621,128]{1,0:T(8,128)(2,1)} %bitcast.7, ...), custom_call_target="tpu_custom_call" | custom-call | tf_op jit(solution)/shard_map/pallas_call | solution.py:688
  51.8 1.8 %copy.17 = bf16[8,12,2304]{2,0,1:T(8,128)(2,1)} copy(bf16[8,12,2304]{2,0,1:T(8,128)(2,1)} %bitcast.4) | data formatting | bytes 884736

commit v7 on v6

--- a/solution.py
+++ b/solution.py
@@ -30,7 +30,7 @@
 LON = 16
 BIG = 1e30
 SCALE = HEAD_DIM**-0.5
-PAIR = 2
+PAIR = 4
 
 
 def slot_positions():
@@ -555,16 +555,15 @@
         put_rows(target, piece(p, strip, half), source.astype(jnp.float32)[:HALF])
 
     def step(at, carry):
-        stage, pair = at // 2, lax.rem(at, 2)
-        block = stage // 2
-        lat_window = jnp.where(block == 0, stage, 3 - stage)
-
-        @pl.when(lax.rem(at, 4) == 0)
+        block = at // 2
+        lat_window = jnp.where(block == 0, at, 3 - at)
+
+        @pl.when(lax.rem(at, 2) == 0)
         def _():
             wait_sibling(block)
             spread_tables(block, gathered, spread, tables)
 
-        @pl.when(at == 4)
+        @pl.when(at == 2)
         def _():
             for p in range(2):
                 widen(x, p, 2, 0, sent[p, 1, 3])
@@ -575,7 +574,7 @@
                 widen(x, p, 3, 0, received[p, 3])
                 widen(x, p, 3, 1, received[p, 4])
 
-        @pl.when(at == 6)
+        @pl.when(at == 3)
         def _():
             for p in range(2):
                 widen(x, p, 0, 0, sent[p, 1, 1])
@@ -586,9 +585,14 @@
                 widen(x, p, 0, 1, received[p, 0])
                 widen(x, p, 1, 1, received[p, 1])
 
-        run_windows(block, lat_window, pair, x, y, tables, consts, weights, lat)
-
-        narrow(block, pair, lat_window)
+        @pl.when(at == 0)
+        def _():
+            pass_on(1)
+
+        run_windows(block, lat_window, lax.rem(at, 1), x, y, tables, consts, weights, lat)
+
+        for p in range(2):
+            narrow(block, p, lat_window)
 
         def after(when, copies):
             @pl.when(at == when)
@@ -596,26 +600,19 @@
                 for copy in copies:
                     copy.start()
 
-        after(1, ahead[0:3])
-        after(2, [ahead[3], ahead[5]])
-        after(3, [ahead[4], ahead[6]])
-        after(4, home[0:3])
-        after(5, home[3:6])
-        after(6, home[6:7])
-        after(7, home[7:8])
+        after(0, ahead[0:3])
+        after(1, ahead[3:7])
+        after(2, home[0:6])
+        after(3, home[6:8])
 
         @pl.when(at == 0)
-        def _():
-            pass_on(1)
-
-        @pl.when(at == 1)
         def _():
             near_part(1)
             far_part(1)
 
         return carry
 
-    lax.fori_loop(0, 8, step, 0)
+    lax.fori_loop(0, 4, step, 0)
 
     def gather_levels(p, from_strip, from_half, strip, half):
         for near in range(4):

time: 53.7 us -> 49 us (0.912)
  Pallas kernels: 51.8 us -> 47.1 us
    pallas_call x1, Pallas kernels: 51.8 us -> 47.1 us  [body(): pl.pallas_call(kernel, out_shape=jax.ShapeDtypeStruct((ROWS, Z, COLS * C)...]
where the time goes in v7:
time: 49 us; the launch traced here: 48.9 us
  Pallas kernels  47.1 us (96%)
  local copies, waits for them, and re-layouts  1.8 us (4%)
    pallas_call x1, Pallas kernels, body(): pl.pallas_call(kernel, out_shape=jax.ShapeDtypeStruct((ROWS, Z, COLS * C)...  47.1 us
    unnamed x1, local copies, waits for them, and re-layouts  1.8 us

profile of v7, /device:TPU:0, one launch (start us, length us, event | category | flops | bytes accessed | tf_op | source)
XLA Modules:
  0.0 48.9 jit_solution(7998709010403281383)
XLA Ops:
  0.0 47.1 %shard_map.145 = bf16[12,8,2304]{2,1,0:T(8,128)(2,1)} custom-call(bf16[12,8,2304]{2,1,0:T(8,128)(2,1)} %bitcast.5, s32[12,12]{1,0:T(8,128)} %ids.1, s32[2]{0:T(128)} %types.1, bf16[3,192]{1,0:T(4,128)(2,1)} %embed_in.1, bf16[621,128]{1,0:T(8,128)(2,1)} %bitcast.6, bf16[621,128]{1,0:T(8,128)(2,1)} %bitcast.7, ...), custom_call_target="tpu_custom_call" | custom-call | tf_op jit(solution)/shard_map/pallas_call | solution.py:685
  47.1 1.8 %copy.17 = bf16[8,12,2304]{2,0,1:T(8,128)(2,1)} copy(bf16[8,12,2304]{2,0,1:T(8,128)(2,1)} %bitcast.4) | data formatting | bytes 884736
